TPU v7x, 256 devices: a whole 4x4x8 slice. The times are simulated.
256 devices in a mesh: row: 32 (over x, z_lo, y), col: 8 (over z_hi, core).
Axes of the slice: x: 4, y: 4, z: 8 (z_hi: 4, z_lo: 2; z = z_hi * 2 + z_lo), core: 2. Of those that a mesh axis runs over, the one named last changes fastest.
Arguments:
- object_field: float32 [2, 16384, 4096], P(None, 'row', 'col'), may hold values from -13 to 13
- probe_modes: float32 [2, 2, 256, 256], replicated, may hold values from -5 to 5
- scan_offsets: int32 [32, 8, 2, 6], P('row', 'col'), may hold values from 0 to 16128, as said below
- scan_counts: int32 [32, 8], P('row', 'col'), may hold values from 1 to 6, as said below
- amplitudes: bfloat16 [32, 8, 6, 256, 256], P('row', 'col'), may hold values from 0 to 2.5
Outputs:
- object_new: float32 [2, 16384, 4096], P(None, 'row', 'col')
- probe_new: float32 [2, 2, 256, 256], replicated
Inputs may be any that keep to these rules, and one draw needn't show every extreme that they name: `scan_counts`: some tile has exactly 6 live positions. `scan_offsets`: each patch of 256 x 256 pixels lies inside the object, and its centre (top-left plus 256 // 2 in each direction) lies in the slot's own tile.
All inputs are finite; a program needn't handle non-finite values.
Results may differ from a plain program's by a relative error of at most 0.0003.
Values sent between devices are 32-bit elements; how exact they have to be, the bound alone decides.
A program may use at most 64 MiB of HBM per device.

v0:
```python
import math

import jax
import jax.numpy as jnp
from jax import lax
from jax.sharding import PartitionSpec as P

HIGHEST = lax.Precision.HIGHEST


def extended_2(cells, sides, width):
    for axis, dim in sides:
        count = lax.axis_size(axis)
        ends = count - 1
        head = lax.slice_in_dim(cells, 0, width, axis=dim)
        tail = lax.slice_in_dim(cells, cells.shape[dim] - width, cells.shape[dim], axis=dim)
        cells = jnp.concatenate(
            [
                lax.ppermute(tail, axis, [(i, (i + 1) % count) for i in range(ends)]),
                cells,
                lax.ppermute(head, axis, [((i + 1) % count, i) for i in range(ends)]),
            ],
            axis=dim,
        )
    return cells


def dft_tables(edge_size):
    counter = jnp.arange(edge_size, dtype=jnp.int32)
    phases = counter[:, None] * counter[None, :] % edge_size
    angles = phases.astype(jnp.float32) * (2.0 * math.pi / edge_size)
    return jnp.concatenate([jnp.cos(angles), jnp.sin(angles)], axis=1)


def combine_parts(cosine_real, cosine_imag, sine_real, sine_imag, inverse):
    if inverse:
        return (cosine_real - sine_imag, cosine_imag + sine_real)
    return (cosine_real + sine_imag, cosine_imag - sine_real)


def transform(real_part, imag_part, table_pair, inverse):
    mode_count = real_part.shape[0]
    edge_size = real_part.shape[-1]
    stacked = jnp.concatenate([real_part, imag_part], axis=0)
    right_pass = jnp.einsum("bij,jk->bik", stacked, table_pair, precision=HIGHEST)
    first_real, first_imag = combine_parts(
        right_pass[:mode_count, :, :edge_size],
        right_pass[mode_count:, :, :edge_size],
        right_pass[:mode_count, :, edge_size:],
        right_pass[mode_count:, :, edge_size:],
        inverse,
    )
    stacked = jnp.concatenate([first_real, first_imag], axis=0)
    left_pass = jnp.einsum("jk,bji->bki", table_pair, stacked, precision=HIGHEST)
    second_real, second_imag = combine_parts(
        left_pass[:mode_count, :edge_size],
        left_pass[mode_count:, :edge_size],
        left_pass[:mode_count, edge_size:],
        left_pass[mode_count:, edge_size:],
        inverse,
    )
    return (second_real / edge_size, second_imag / edge_size)


def fold_rims(padded, tile_rows, tile_cols, margin):
    low = 2 * margin
    row_end = tile_rows + 3 * margin
    col_end = tile_cols + 3 * margin
    inner = padded[:, low : low + tile_rows, low : low + tile_cols]
    inner = inner.at[:, :margin, :].add(padded[:, :margin, low : low + tile_cols])
    inner = inner.at[:, tile_rows - margin :, :].add(padded[:, row_end:, low : low + tile_cols])
    inner = inner.at[:, :, :margin].add(padded[:, low : low + tile_rows, :margin])
    inner = inner.at[:, :, tile_cols - margin :].add(padded[:, low : low + tile_rows, col_end:])
    inner = inner.at[:, :margin, :margin].add(padded[:, :margin, :margin])
    inner = inner.at[:, :margin, tile_cols - margin :].add(padded[:, :margin, col_end:])
    inner = inner.at[:, tile_rows - margin :, :margin].add(padded[:, row_end:, :margin])
    inner = inner.at[:, tile_rows - margin :, tile_cols - margin :].add(
        padded[:, row_end:, col_end:]
    )
    return inner


def on_device(object_field, probe_modes, scan_offsets, scan_counts, amplitudes):
    tile_rows = object_field.shape[1]
    tile_cols = object_field.shape[2]
    mode_count = probe_modes.shape[1]
    edge_size = probe_modes.shape[-1]
    margin = edge_size // 2
    anchor_row = lax.axis_index("row") * tile_rows
    anchor_col = lax.axis_index("col") * tile_cols
    extended = extended_2(object_field, (("row", 1), ("col", 2)), margin)
    table_pair = dft_tables(edge_size)
    probe_real = probe_modes[0]
    probe_imag = probe_modes[1]
    probe_power = jnp.sum(probe_real * probe_real + probe_imag * probe_imag, axis=0)
    live_count = scan_counts[0, 0]

    def slot_terms(position):
        row_start = scan_offsets[0, 0, 0, position] - anchor_row + margin
        col_start = scan_offsets[0, 0, 1, position] - anchor_col + margin
        patch_field = lax.dynamic_slice(
            extended, (0, row_start, col_start), (2, edge_size, edge_size)
        )
        patch_real = patch_field[0]
        patch_imag = patch_field[1]
        wave_real = probe_real * patch_real - probe_imag * patch_imag
        wave_imag = probe_real * patch_imag + probe_imag * patch_real
        far_real, far_imag = transform(wave_real, wave_imag, table_pair, False)
        intensity = jnp.sum(far_real * far_real + far_imag * far_imag, axis=0)
        factor = (
            amplitudes[0, 0, position].astype(jnp.float32) / jnp.sqrt(jnp.maximum(intensity, 0.25))
            - 1.0
        )
        back_real, back_imag = transform(far_real * factor, far_imag * factor, table_pair, True)
        update = jnp.stack(
            [
                jnp.sum(probe_real * back_real + probe_imag * back_imag, axis=0),
                jnp.sum(probe_real * back_imag - probe_imag * back_real, axis=0),
            ]
        )
        probe_term = jnp.stack(
            [
                patch_real * back_real + patch_imag * back_imag,
                patch_real * back_imag - patch_imag * back_real,
            ]
        )
        power_term = patch_real * patch_real + patch_imag * patch_imag
        return (row_start, col_start, update, probe_term, power_term)

    def add_window(canvas, values, row_start, col_start):
        window = lax.dynamic_slice(canvas, (0, row_start, col_start), values.shape)
        return lax.dynamic_update_slice(canvas, window + values, (0, row_start, col_start))

    gradient = jnp.zeros((2, tile_rows + edge_size, tile_cols + edge_size), jnp.float32)
    probe_grad = jnp.zeros((2, mode_count, edge_size, edge_size), jnp.float32)
    probe_norm = jnp.zeros((edge_size, edge_size), jnp.float32)

    def visit_lit(position, state_tuple):
        gradient_now, lighting_now, grad_now, norm_now = state_tuple
        row_start, col_start, update, probe_term, power_term = slot_terms(position)
        gradient_now = add_window(gradient_now, update, row_start, col_start)
        lighting_now = add_window(lighting_now, probe_power[None], row_start, col_start)
        return (gradient_now, lighting_now, grad_now + probe_term, norm_now + power_term)

    lighting = jnp.zeros((1, tile_rows + edge_size, tile_cols + edge_size), jnp.float32)
    gradient, lighting, probe_grad, probe_norm = lax.fori_loop(
        0, live_count, visit_lit, (gradient, lighting, probe_grad, probe_norm)
    )
    stacked = jnp.concatenate([gradient, lighting], axis=0)
    padded = extended_2(stacked, (("row", 1), ("col", 2)), margin)
    folded = fold_rims(padded, tile_rows, tile_cols, margin)
    object_grad = folded[:2]
    lighting_sum = folded[2]
    object_new = object_field + object_grad / (lighting_sum + 1.0)[None]
    total_grad, total_norm = lax.psum((probe_grad, probe_norm), ("row", "col"))
    probe_new = probe_modes + total_grad / (total_norm + 1.0)
    return (object_new, probe_new)


def solution(mesh):
    in_specs = (
        P(None, "row", "col"),
        P(),
        P("row", "col", None, None),
        P("row", "col"),
        P("row", "col", None, None, None),
    )
    out_specs = (P(None, "row", "col"), P())
    return jax.shard_map(
        on_device, mesh=mesh, in_specs=in_specs, out_specs=out_specs, check_vma=False
    )
```

profile of v0, /device:TPU:1, one launch (start us, length us, event | category | flops | bytes accessed | tf_op | source)
XLA Modules:
  0.0 613.0 jit_solution(7151263142433317116)
XLA Ops:
  7.2 1.9 copy.47
  9.2 4.1 collective-permute-start
  13.3 1.3 collective-permute-start.1
  14.6 9.2 %collective-permute-done = f32[2,128,512]{1,2,0:T(8,128)S(1)} collective-permute-done((f32[2,128,512]{1,2,0:T(8,128)S(1)}, f32[2,128,512]{1,2,0:T(8,128)S(1)}, u32[]{:S(2)}, u32[]{:S(2)}) %collective-permute-start) | collective-permute-done | bytes 524320 | tf_op jit(solution)/shard_map/ppermute | solution.py:19
  23.8 3.8 collective-permute-done.1
  27.7 1.3 pad_maximum_fusion.6
  29.0 6.8 %collective-permute-start.2 = (f32[2,768,128]{1,2,0:T(8,128)}, f32[2,768,128]{1,2,0:T(8,128)}, u32[]{:S(2)}, u32[]{:S(2)}) collective-permute-start(f32[2,768,128]{1,2,0:T(8,128)} %get-tuple-element.466), channel_id=1, source_target_pairs={{0,1},{1,2},{2,3},{3,4},{4,5},{5,6},{6,7},{8,9},{9,10},{10,11},{11... | collective-permute-start | bytes 2359304 | tf_op jit(solution)/shard_map/ppermute | solution.py:19
  35.8 1.9 collective-permute-start.3
  38.9 2.2 add_reduce_fusion.2
  41.1 4.0 collective-permute-done.2
  45.1 13.7 %collective-permute-done.3 = f32[2,768,128]{1,2,0:T(8,128)} collective-permute-done((f32[2,768,128]{1,2,0:T(8,128)}, f32[2,768,128]{1,2,0:T(8,128)}, u32[]{:S(2)}, u32[]{:S(2)}) %collective-permute-start.3) | collective-permute-done | bytes 786464 | tf_op jit(solution)/shard_map/ppermute | solution.py:21
  58.8 3.5 pad_maximum_fusion
  62.2 2.5 broadcast_in_dim.25.clone
  64.7 1.5 broadcast_in_dim.26
  68.0 85.8 %while.27 = (s32[]{:T(128)}, f32[2,768,768]{2,1,0:T(8,128)}, f32[1,768,768]{2,1,0:T(8,128)}, f32[2,2,256,256]{3,2,1,0:T(8,128)}, f32[256,256]{0,1:T(8,128)}, /*i...) while((s32[]{:T(128)}, f32[2,768,768]{2,1,0:T(8,128)}, ...), condition=%wide.region_5.6_spmd, body=%wide.region_1.5_spmd.sunk | while | flops 6450118656 | bytes 70124120 | solution.py:146
  70.9 2.1 add_add_fusion.2
  74.0 2.3 multiply_subtract_fusion.2
  76.2 1.8 fusion.63
  78.2 1.8 convolution_bitcast_fusion.4
  80.9 1.6 constant_dynamic-slice_fusion.7
  84.6 1.8 fusion.65
  86.6 1.8 convolution_bitcast_fusion.5
  88.5 1.3 add_bitcast_fusion.2
  90.2 3.0 add_reduce_fusion.6
  93.2 1.6 copy.77
  94.8 1.3 maximum_add_fusion.5
  96.1 1.3 copy.78
  98.9 6.6 %dynamic_update_slice.16 = f32[2,768,768]{2,1,0:T(8,128)} dynamic-update-slice(f32[2,768,768]{2,1,0:T(8,128)} %get-tuple-element.634, f32[2,256,256]{2,1,0:T(8,128)S(1)} %copy.76, s32[]{:T(128)} %constant.306.clone.1..sunk, s32[]{:T(128)S(6)} %select_n.54, s32[]{:T(128)S(6)} %select_n.55) | dynamic-update-slice | bytes 1048580 | tf_op jit(solution)/shard_map/while/body/dynamic_update_slice | solution.py:132
  105.5 1.1 bitcast_add_fusion.2
  106.6 3.8 dynamic_update_slice.17
  113.1 2.1 add_add_fusion.2
  116.2 2.3 multiply_subtract_fusion.2
  118.5 1.8 fusion.63
  120.4 1.8 convolution_bitcast_fusion.4
  123.1 1.6 constant_dynamic-slice_fusion.7
  126.9 1.8 fusion.65
  128.9 1.8 convolution_bitcast_fusion.5
  130.8 1.3 add_bitcast_fusion.2
  132.5 3.0 add_reduce_fusion.6
  135.4 1.6 copy.77
  137.0 1.3 maximum_add_fusion.5
  138.3 1.3 copy.78
  141.2 6.8 %dynamic_update_slice.16 = f32[2,768,768]{2,1,0:T(8,128)} dynamic-update-slice(f32[2,768,768]{2,1,0:T(8,128)} %get-tuple-element.634, f32[2,256,256]{2,1,0:T(8,128)S(1)} %copy.76, s32[]{:T(128)} %constant.306.clone.1..sunk, s32[]{:T(128)S(6)} %select_n.54, s32[]{:T(128)S(6)} %select_n.55) | dynamic-update-slice | bytes 1048580 | tf_op jit(solution)/shard_map/while/body/dynamic_update_slice | solution.py:132
  147.9 1.1 bitcast_add_fusion.2
  149.1 3.9 dynamic_update_slice.17
  153.9 2.8 constant_dynamic-update-slice_fusion.1
  157.1 2.9 copy-done.6
  160.0 1.2 fusion.41
  161.2 1.4 collective-permute-start.4
  162.6 1.3 collective-permute-start.5
  163.9 12.0 %collective-permute-done.4 = f32[3,128,768]{2,1,0:T(8,128)S(1)} collective-permute-done((f32[3,128,768]{2,1,0:T(8,128)}, f32[3,128,768]{2,1,0:T(8,128)S(1)}, u32[]{:S(2)}, u32[]{:S(2)}) %collective-permute-start.4) | collective-permute-done | bytes 1179680 | tf_op jit(solution)/shard_map/ppermute | solution.py:19
  175.9 4.5 collective-permute-done.5
  180.5 4.0 pad_maximum_fusion.1
  184.4 47.6 %collective-permute-start.6 = (f32[3,1024,128]{2,1,0:T(8,128)}, f32[3,1024,128]{2,1,0:T(8,128)}, u32[]{:S(2)}, u32[]{:S(2)}) collective-permute-start(f32[3,1024,128]{2,1,0:T(8,128)} %get-tuple-element.463), channel_id=1, source_target_pairs={{0,1},{1,2},{2,3},{3,4},{4,5},{5,6},{6,7},{8,9},{9,10},{10,11},{11... | collective-permute-start | bytes 4718600 | tf_op jit(solution)/shard_map/ppermute | solution.py:19
  232.1 1.9 collective-permute-start.7
  235.3 2.2 slice.451
  237.6 349.0 %all-reduce.3.cloned.1.call-done = (f32[2,2,256,256]{3,2,1,0:T(8,128)}, f32[256,256]{0,1:T(8,128)}) async-done(((f32[2,2,256,256]{3,2,1,0:T(8,128)}, f32[256,256]{0,1:T(8,128)}), (f32[2,2,256,256]{3,2,1,0:T(8,128)}, f32[256,256]{0,1:T(8,128)})) %all-reduce.3.cloned.1.call-update) | async-done | bytes 1310736 | tf_op jit(solution)/shard_map/psum | solution.py:155
  588.4 2.9 divide_add_fusion
  591.2 1.3 fusion.29
  592.7 1.3 fusion.27
  594.0 1.3 fusion.26
  596.3 3.0 add_select_fusion.1
  599.3 2.6 scatter-add.35
  604.2 2.0 fusion.24
  (110 shorter events, 23.8 us)
Async XLA Ops:
  7.2 579.4 %all-reduce.3.cloned.1.call-start = ((), (), s32[]{:S(2)}) async-start(), calls=%async_computation | async-start | bytes 2621440 | tf_op jit(solution)/shard_map/psum | solution.py:155
  9.1 19.9 %copy-start.7 = (f32[2,512,512]{1,2,0:T(8,128)}, f32[2,512,512]{1,2,0:T(8,128)S(1)}, u32[]{:S(2)}) copy-start(f32[2,512,512]{1,2,0:T(8,128)S(1)} %copy.47) | copy-start | bytes 6291460
  9.2 14.6 %collective-permute-start = (f32[2,128,512]{1,2,0:T(8,128)S(1)}, f32[2,128,512]{1,2,0:T(8,128)S(1)}, u32[]{:S(2)}, u32[]{:S(2)}) collective-permute-start(f32[2,128,512]{1,2,0:T(8,128)S(1)} %get-tuple-element.468), channel_id=1, source_target_pairs={{0,8},{8,16},{16,24},{24,32},{32,40},{40,48},{48,56},{56,64},{64,7... | collective-permute-start | bytes 1572872 | tf_op jit(solution)/shard_map/ppermute | solution.py:19
  13.3 14.4 %collective-permute-start.1 = (f32[2,128,512]{1,2,0:T(8,128)S(1)}, f32[2,128,512]{1,2,0:T(8,128)S(1)}, u32[]{:S(2)}, u32[]{:S(2)}) collective-permute-start(f32[2,128,512]{1,2,0:T(8,128)S(1)} %get-tuple-element.469), channel_id=1, source_target_pairs={{8,0},{16,8},{24,16},{32,24},{40,32},{48,40},{56,48},{64,56},{72,6... | collective-permute-start | bytes 1572872 | tf_op jit(solution)/shard_map/ppermute | solution.py:21
  23.8 5.2 copy-start.17
  27.7 1.3 copy-start.19
  29.0 12.0 %copy-start.10 = (f32[2,2,256,256]{3,2,1,0:T(8,128)S(1)}, f32[2,2,256,256]{3,2,1,0:T(8,128)}, u32[]{:S(2)}) copy-start(f32[2,2,256,256]{3,2,1,0:T(8,128)} %param.24) | copy-start | bytes 3145732
  29.0 16.1 %collective-permute-start.2 = (f32[2,768,128]{1,2,0:T(8,128)}, f32[2,768,128]{1,2,0:T(8,128)}, u32[]{:S(2)}, u32[]{:S(2)}) collective-permute-start(f32[2,768,128]{1,2,0:T(8,128)} %get-tuple-element.466), channel_id=1, source_target_pairs={{0,1},{1,2},{2,3},{3,4},{4,5},{5,6},{6,7},{8,9},{9,10},{10,11},{11... | collective-permute-start | bytes 2359304 | tf_op jit(solution)/shard_map/ppermute | solution.py:19
  35.8 23.0 %collective-permute-start.3 = (f32[2,768,128]{1,2,0:T(8,128)}, f32[2,768,128]{1,2,0:T(8,128)}, u32[]{:S(2)}, u32[]{:S(2)}) collective-permute-start(f32[2,768,128]{1,2,0:T(8,128)} %get-tuple-element.467), channel_id=1, source_target_pairs={{1,0},{2,1},{3,2},{4,3},{5,4},{6,5},{7,6},{9,8},{10,9},{11,10},{12... | collective-permute-start | bytes 2359304 | tf_op jit(solution)/shard_map/ppermute | solution.py:21
  38.8 20.0 %copy-start.8 = (f32[2,512,512]{1,2,0:T(8,128)S(1)}, f32[2,512,512]{1,2,0:T(8,128)}, u32[]{:S(2)}) copy-start(f32[2,512,512]{1,2,0:T(8,128)} %copy-done.7) | copy-start | bytes 6291460
  38.8 20.0 %copy-start.18 = (f32[2,128,512]{1,2,0:T(8,128)S(1)}, f32[2,128,512]{1,2,0:T(8,128)}, u32[]{:S(2)}) copy-start(f32[2,128,512]{1,2,0:T(8,128)} %copy-done.17) | copy-start | bytes 1572868
  38.8 20.0 %copy-start.20 = (f32[2,128,512]{1,2,0:T(8,128)S(1)}, f32[2,128,512]{1,2,0:T(8,128)}, u32[]{:S(2)}) copy-start(f32[2,128,512]{1,2,0:T(8,128)} %copy-done.19) | copy-start | bytes 1572868
  64.7 3.3 copy-start.21
  68.9 7.3 %copy-start = (f32[2,256,256]{2,1,0:T(8,128)}, f32[2,256,256]{2,1,0:T(8,128)S(1)}, u32[]{:S(2)}) copy-start(f32[2,256,256]{2,1,0:T(8,128)S(1)} %get-tuple-element.664) | copy-start | bytes 1572868 | tf_op jit(solution)/shard_map/while
  73.0 3.2 copy-start.3
  86.6 1.9 copy-start.4
  88.5 1.5 copy-start.1
  96.1 1.3 copy-start.5
  97.4 8.1 %copy-start.11 = (f32[256,256]{1,0:T(8,128)S(1)}, f32[256,256]{1,0:T(8,128)}, u32[]{:S(2)}) copy-start(f32[256,256]{1,0:T(8,128)} %get-tuple-element.668) | copy-start | bytes 786436 | tf_op jit(solution)/shard_map/while
  97.6 12.8 %copy-start.2 = (f32[2,256,256]{2,1,0:T(8,128)S(1)}, f32[2,256,256]{2,1,0:T(8,128)}, u32[]{:S(2)}) copy-start(f32[2,256,256]{2,1,0:T(8,128)} %copy-done) | copy-start | bytes 1572868 | tf_op jit(solution)/shard_map/while
  111.1 7.3 %copy-start = (f32[2,256,256]{2,1,0:T(8,128)}, f32[2,256,256]{2,1,0:T(8,128)S(1)}, u32[]{:S(2)}) copy-start(f32[2,256,256]{2,1,0:T(8,128)S(1)} %get-tuple-element.664) | copy-start | bytes 1572868 | tf_op jit(solution)/shard_map/while
  115.2 3.2 copy-start.3
  128.9 1.9 copy-start.4
  130.8 1.5 copy-start.1
  138.3 1.3 copy-start.5
  139.7 8.3 %copy-start.11 = (f32[256,256]{1,0:T(8,128)S(1)}, f32[256,256]{1,0:T(8,128)}, u32[]{:S(2)}) copy-start(f32[256,256]{1,0:T(8,128)} %get-tuple-element.668) | copy-start | bytes 786436 | tf_op jit(solution)/shard_map/while
  139.9 13.1 %copy-start.2 = (f32[2,256,256]{2,1,0:T(8,128)S(1)}, f32[2,256,256]{2,1,0:T(8,128)}, u32[]{:S(2)}) copy-start(f32[2,256,256]{2,1,0:T(8,128)} %copy-done) | copy-start | bytes 1572868 | tf_op jit(solution)/shard_map/while
  153.9 3.1 copy-start.9
  157.1 2.9 copy-start.6
  161.2 14.7 %collective-permute-start.4 = (f32[3,128,768]{2,1,0:T(8,128)}, f32[3,128,768]{2,1,0:T(8,128)S(1)}, u32[]{:S(2)}, u32[]{:S(2)}) collective-permute-start(f32[3,128,768]{2,1,0:T(8,128)} %get-tuple-element.465), channel_id=1, source_target_pairs={{0,8},{8,16},{16,24},{24,32},{32,40},{40,48},{48,56},{56,64},{64,7... | collective-permute-start | bytes 3538952 | tf_op jit(solution)/shard_map/ppermute | solution.py:19
  162.6 17.9 %collective-permute-start.5 = (f32[3,128,768]{2,1,0:T(8,128)S(1)}, f32[3,128,768]{2,1,0:T(8,128)S(1)}, u32[]{:S(2)}, u32[]{:S(2)}) collective-permute-start(f32[3,128,768]{2,1,0:T(8,128)S(1)} %get-tuple-element.464), channel_id=1, source_target_pairs={{8,0},{16,8},{24,16},{32,24},{40,32},{48,40},{56,48},{64,56},{72,6... | collective-permute-start | bytes 3538952 | tf_op jit(solution)/shard_map/ppermute | solution.py:21
  163.9 70.7 %copy-start.22 = (s32[3]{0:T(128)S(1)}, s32[3]{0:T(128)}, u32[]{:S(2)}) copy-start(s32[3]{0:T(128)} %constant.317.clone.1) | copy-start | bytes 40
  175.9 8.5 %copy-start.13 = (f32[3,128,768]{2,1,0:T(8,128)}, f32[3,128,768]{2,1,0:T(8,128)S(1)}, u32[]{:S(2)}) copy-start(f32[3,128,768]{2,1,0:T(8,128)S(1)} %collective-permute-done.4) | copy-start | bytes 3538948
  180.5 4.0 copy-start.15
  184.4 408.3 %collective-permute-start.6 = (f32[3,1024,128]{2,1,0:T(8,128)}, f32[3,1024,128]{2,1,0:T(8,128)}, u32[]{:S(2)}, u32[]{:S(2)}) collective-permute-start(f32[3,1024,128]{2,1,0:T(8,128)} %get-tuple-element.463), channel_id=1, source_target_pairs={{0,1},{1,2},{2,3},{3,4},{4,5},{5,6},{6,7},{8,9},{9,10},{10,11},{11... | collective-permute-start | bytes 4718600 | tf_op jit(solution)/shard_map/ppermute | solution.py:19
  232.1 361.9 %collective-permute-start.7 = (f32[3,1024,128]{2,1,0:T(8,128)}, f32[3,1024,128]{2,1,0:T(8,128)}, u32[]{:S(2)}, u32[]{:S(2)}) collective-permute-start(f32[3,1024,128]{2,1,0:T(8,128)} %get-tuple-element.462), channel_id=1, source_target_pairs={{1,0},{2,1},{3,2},{4,3},{5,4},{6,5},{7,6},{9,8},{10,9},{11,10},{12... | collective-permute-start | bytes 4718600 | tf_op jit(solution)/shard_map/ppermute | solution.py:21
  588.4 2.9 copy-start.14
  588.4 4.1 copy-start.16
  602.0 2.2 copy-start.12
Sparse Core Ops, SparseCore 0:
  164.0 422.4 all-reduce.2
where the time goes:
time: 617 us; the launch traced here: 613 us
  waiting for transfers between devices  396 us (64%)
  starting transfers between devices  66.3 us (11%)
  local copies, waits for them, and re-layouts  58.4 us (9%)
  other arithmetic  57.7 us (9%)
  matrix products  14.7 us (2%)
  between operations  14.3 us (2%)
    psum x1, waiting for transfers between devices, on_device(): total_grad, total_norm = lax.psum((probe_grad, probe_norm), ('row', 'col'))  349 us
    ppermute x4, starting transfers between devices, extended_2(): lax.ppermute(tail, axis, [(i, (i + 1) % count) for i in range(ends)])  59.8 us
    ppermute x4, waiting for transfers between devices, extended_2(): lax.ppermute(tail, axis, [(i, (i + 1) % count) for i in range(ends)])  25.2 us
    ppermute x4, waiting for transfers between devices, extended_2(): lax.ppermute(head, axis, [((i + 1) % count, i) for i in range(ends)])  22 us
    dynamic_update_slice x6, local copies, waits for them, and re-layouts, add_window(): lax.dynamic_update_slice(canvas, window + values, (0, row_start, col_start))  21.4 us
  transfers between devices with their start and end apart: 9, of which 7 were waited for; matrix products, arithmetic and copies ran while one was open for 3% of the time, Pallas kernels for 0%

commit v1 on v0

v1 whole, which is shorter than its diff:
```python
import functools
import math

import jax
import jax.numpy as jnp
import numpy as np
from jax import lax
from jax.experimental import pallas as pl
from jax.experimental.pallas import tpu as pltpu
from jax.sharding import PartitionSpec as P

MESH = pl.DeviceIdType.MESH
EDGE = 256
HALF = 128
TILE = 512
MARGIN = 128
EXT = TILE + 2 * MARGIN
SLOTS = 6
SIDES = tuple((dr, dc) for dr in (-1, 0, 1) for dc in (-1, 0, 1))
NEIGHBOURS = ((0, 1), (0, -1), (1, 1), (1, -1), (-1, 1), (-1, -1), (1, 0), (-1, 0))
LIT = 1024
LIT_PAD = LIT + 128
ROWS = 32


def shifted(dr, dc):
    rows, cols = lax.axis_size("row"), lax.axis_size("col")
    row = lax.rem(lax.axis_index("row") + dr + rows, rows)
    col = lax.rem(lax.axis_index("col") + dc + cols, cols)
    return (row, col)


def edge_span(step):
    if step == 0:
        return pl.ds(0, TILE), pl.ds(MARGIN, TILE)
    if step > 0:
        return pl.ds(TILE - MARGIN, MARGIN), pl.ds(0, MARGIN)
    return pl.ds(0, MARGIN), pl.ds(MARGIN + TILE, MARGIN)


def halo_kernel(field, meta, framed, metas, local_sems, send_sems, recv_sems, meta_send, meta_recv):
    barrier = pltpu.get_barrier_semaphore()
    for dr, dc in NEIGHBOURS:
        pl.semaphore_signal(barrier, inc=1, device_id=shifted(dr, dc), device_id_type=MESH)
    own = pltpu.make_async_copy(
        field, framed.at[:, pl.ds(MARGIN, TILE), pl.ds(MARGIN, TILE)], local_sems.at[0]
    )
    own_meta = pltpu.make_async_copy(meta, metas.at[4], local_sems.at[1])
    pl.semaphore_wait(barrier, len(NEIGHBOURS))
    copies = []
    for n, (dr, dc) in enumerate(NEIGHBOURS):
        src_r, dst_r = edge_span(dr)
        src_c, dst_c = edge_span(dc)
        copies.append(
            pltpu.make_async_remote_copy(
                src_ref=field.at[:, src_r, src_c],
                dst_ref=framed.at[:, dst_r, dst_c],
                send_sem=send_sems.at[n],
                recv_sem=recv_sems.at[n],
                device_id=shifted(dr, dc),
                device_id_type=MESH,
            )
        )
        copies.append(
            pltpu.make_async_remote_copy(
                src_ref=meta,
                dst_ref=metas.at[SIDES.index((-dr, -dc))],
                send_sem=meta_send.at[n],
                recv_sem=meta_recv.at[n],
                device_id=shifted(dr, dc),
                device_id_type=MESH,
            )
        )
    for copy in copies:
        copy.start()
    own.start()
    own_meta.start()
    own.wait()
    own_meta.wait()
    for copy in copies:
        copy.wait()


def gather_frame(field, meta):
    any_spec = pl.BlockSpec(memory_space=pl.ANY)
    count = len(NEIGHBOURS)
    return pl.pallas_call(
        halo_kernel,
        out_shape=(
            jax.ShapeDtypeStruct((2, EXT, EXT), jnp.float32),
            jax.ShapeDtypeStruct((9, 8, 128), jnp.int32),
        ),
        in_specs=[any_spec, any_spec],
        out_specs=(any_spec, any_spec),
        scratch_shapes=[
            pltpu.SemaphoreType.DMA((2,)),
            pltpu.SemaphoreType.DMA((count,)),
            pltpu.SemaphoreType.DMA((count,)),
            pltpu.SemaphoreType.DMA((count,)),
            pltpu.SemaphoreType.DMA((count,)),
        ],
        compiler_params=pltpu.CompilerParams(
            collective_id=0, has_side_effects=True, vmem_limit_bytes=4 * 1024 * 1024
        ),
        name="halo",
    )(field, meta)


def split(x):
    high = x.astype(jnp.bfloat16)
    return high, (x - high.astype(jnp.float32)).astype(jnp.bfloat16)


def tables():
    n = np.arange(HALF)
    angle = 2.0 * np.pi * ((n[:, None] * n[None, :]) % HALF) / HALF
    cosine, sine = np.cos(angle), np.sin(angle)
    right = np.block([[cosine, -sine], [sine, cosine]]).astype(np.float32)
    half_angle = 2.0 * np.pi * n / EDGE
    twist = np.stack([np.cos(half_angle), np.sin(half_angle)]).astype(np.float32)
    lanes = np.broadcast_to(twist[:, None, :], (2, 8, HALF))
    subs = np.broadcast_to(twist[:, :, None], (2, HALF, HALF))
    order = np.concatenate([np.arange(0, EDGE, 2), np.arange(1, EDGE, 2)])
    pick = (order[:, None] == np.arange(EDGE)[None, :]).astype(np.float32)
    out = []
    for table in (right, right.T):
        high = table.astype(jnp.bfloat16)
        out += [high, (table - high.astype(np.float32)).astype(jnp.bfloat16)]
    out += [pick.astype(jnp.bfloat16), pick.T.astype(jnp.bfloat16), lanes.copy(), subs.copy()]
    return [jnp.asarray(t) for t in out]


def cat(parts, axis):
    return jnp.concatenate(parts, axis=axis)


def tile_kernel(
    place, metas, framed, probe, amps, rh, rl, lh, ll, pick, pick_t, lane_tw, sub_tw,
    grad, shade, sums,
    patch, xh, xl, yh, yl, amp, light, power,
):
    f32, bf16 = jnp.float32, jnp.bfloat16
    dot = functools.partial(jnp.dot, preferred_element_type=f32)
    lane = lax.broadcasted_iota(jnp.int32, (1, HALF), 1)
    top, left = place[0], place[1]

    grad[...] = jnp.zeros_like(grad)
    sums[...] = jnp.zeros_like(sums)
    for i in range(0, EDGE, ROWS):
        s = pl.ds(i, ROWS)
        power[s, :] = sum(probe[c, k, s, :] * probe[c, k, s, :] for k in range(2) for c in range(2))
    light[pl.ds(256, TILE), pl.ds(256, TILE)] = jnp.zeros((TILE, TILE), f32)

    def spread(low, high, down, shift):
        below = jnp.zeros((8, HALF), f32)
        low, high = (
            pltpu.roll(pltpu.roll(cat([v, below], 0), down, 0), shift, 1) for v in (low, high)
        )
        keep = lane >= shift
        return (
            jnp.where(keep, low, 0.0),
            jnp.where(keep, high, low),
            jnp.where(keep, 0.0, high),
        )

    def light_slot(which, position):
        r = metas[which, 0, position] - top + 256
        c = metas[which, 0, SLOTS + position] - left + 256

        @pl.when((r > 0) & (r < 768) & (c > 0) & (c < 768))
        def _():
            shift, down = lax.rem(c, HALF), lax.rem(r, 8)
            base = pl.multiple_of(c - shift, HALF)
            first = pl.multiple_of(r - down, 8)
            for i in range(0, EDGE, ROWS):
                s = pl.ds(i, ROWS)
                blocks = spread(power[s, :HALF], power[s, HALF:], down, shift)
                for b, block in enumerate(blocks):
                    at = (pl.ds(first + i, ROWS + 8), pl.ds(base + b * HALF, HALF))
                    light[at] += block

    def light_tile(which, _):
        def one(position, _):
            light_slot(which, position)
            return 0

        lax.fori_loop(0, metas[which, 0, 2 * SLOTS], one, 0)
        return 0

    lax.fori_loop(0, 9, light_tile, 0)
    for i in range(0, TILE, ROWS):
        shade[pl.ds(i, ROWS), :] = 1.0 / (light[pl.ds(256 + i, ROWS), pl.ds(256, TILE)] + 1.0)

    right_hhl = cat([rh[...], rh[...], rl[...]], 0)

    def visit(position, _):
        r = metas[4, 0, position] - top + MARGIN
        c = metas[4, 0, SLOTS + position] - left + MARGIN
        shift = lax.rem(c, HALF)
        base = pl.multiple_of(c - shift, HALF)
        down = lax.rem(r, 8)
        first = pl.multiple_of(r - down, 8)
        up = lax.rem(ROWS + 8 - down, ROWS + 8)
        back_shift = lax.rem(HALF - shift, HALF)
        keep = lane < HALF - shift
        picked = dot(pick[...], amps[position]).astype(bf16)
        amp[...] = dot(picked, pick_t[...])

        for i in range(0, EDGE, ROWS):
            s = pl.ds(i, ROWS)
            planes = []
            for plane in range(2):
                rolled = [
                    pltpu.roll(
                        pltpu.roll(
                            framed[
                                plane, pl.ds(first + i, ROWS + 8), pl.ds(base + b * HALF, HALF)
                            ],
                            up,
                            0,
                        )[:ROWS],
                        back_shift,
                        1,
                    )
                    for b in range(3)
                ]
                planes.append(
                    (jnp.where(keep, rolled[0], rolled[1]), jnp.where(keep, rolled[1], rolled[2]))
                )
            for plane in range(2):
                for h in range(2):
                    patch[plane, s, pl.ds(h * HALF, HALF)] = planes[plane][h]
            for k in range(2):
                wr, wi = [], []
                for h in range(2):
                    pr, pi = (probe[p, k, s, pl.ds(h * HALF, HALF)] for p in range(2))
                    wr.append(pr * planes[0][h] - pi * planes[1][h])
                    wi.append(pr * planes[1][h] + pi * planes[0][h])
                cosine, sine = lane_tw[0, :1, :], lane_tw[1, :1, :]
                dr, di = wr[0] - wr[1], wi[0] - wi[1]
                for part, value in (
                    (0, cat([wr[0] + wr[1], wi[0] + wi[1]], 1)),
                    (1, cat([dr * cosine + di * sine, di * cosine - dr * sine], 1)),
                ):
                    high, low = split(value)
                    at = pl.ds((2 * k + part) * EDGE + i, ROWS)
                    xh[at, :] = high
                    xl[at, :] = low

        for k in range(2):
            for i in range(0, HALF, ROWS):
                res = []
                for row in (i, HALF + i):
                    parts = []
                    for part in range(2):
                        at = pl.ds((2 * k + part) * EDGE + row, ROWS)
                        parts.append(dot(cat([xh[at, :], xl[at, :], xh[at, :]], 1), right_hhl))
                    res.append(
                        (
                            cat([parts[0][:, :HALF], parts[1][:, :HALF]], 1),
                            cat([parts[0][:, HALF:], parts[1][:, HALF:]], 1),
                        )
                    )
                (tr, ti), (br, bi) = res
                cosine = cat([sub_tw[0, pl.ds(i, ROWS), :]] * 2, 1)
                sine = cat([sub_tw[1, pl.ds(i, ROWS), :]] * 2, 1)
                dr, di = tr - br, ti - bi
                for part, real, imag in (
                    (0, tr + br, ti + bi),
                    (1, dr * cosine + di * sine, di * cosine - dr * sine),
                ):
                    for start, value in ((0, real), (HALF, imag)):
                        high, low = split(value)
                        at = (2 * k + part, pl.ds(start + i, ROWS), slice(None))
                        yh[at] = high
                        yl[at] = low

        for part in range(2):
            far = [
                dot(
                    cat([lh[...], lh[...], ll[...]], 1),
                    cat([yh[2 * k + part], yl[2 * k + part], yh[2 * k + part]], 0),
                )
                for k in range(2)
            ]
            for i in range(0, HALF, ROWS):
                pieces = [(f[i : i + ROWS], f[HALF + i : HALF + i + ROWS]) for f in far]
                total = sum(a * a + b * b for a, b in pieces)
                total = jnp.maximum(total * (1.0 / 65536.0), 0.25)
                factor = amp[pl.ds(part * HALF + i, ROWS), :] * lax.rsqrt(total) - 1.0
                factor = factor * (1.0 / 65536.0)
                for k in range(2):
                    for start, value in ((0, pieces[k][0]), (HALF, pieces[k][1])):
                        high, low = split(value * factor)
                        at = (2 * k + part, pl.ds(start + i, ROWS), slice(None))
                        yh[at] = high
                        yl[at] = low
        for k in range(2):
            near = [
                dot(
                    cat([rh[...], rh[...], rl[...]], 1),
                    cat([yh[2 * k + part], yl[2 * k + part], yh[2 * k + part]], 0),
                )
                for part in range(2)
            ]
            for i in range(0, HALF, ROWS):
                (ar, ai), (br, bi) = ((f[i : i + ROWS], f[HALF + i : HALF + i + ROWS]) for f in near)
                cosine = cat([sub_tw[0, pl.ds(i, ROWS), :]] * 2, 1)
                sine = cat([sub_tw[1, pl.ds(i, ROWS), :]] * 2, 1)
                br, bi = br * cosine - bi * sine, bi * cosine + br * sine
                for row, real, imag in ((i, ar + br, ai + bi), (HALF + i, ar - br, ai - bi)):
                    for part in range(2):
                        cols = slice(part * HALF, (part + 1) * HALF)
                        high, low = split(cat([real[:, cols], imag[:, cols]], 1))
                        at = pl.ds((2 * k + part) * EDGE + row, ROWS)
                        xh[at, :] = high
                        xl[at, :] = low

        left_hhl = cat([lh[...], lh[...], ll[...]], 0)
        for i in range(0, EDGE, ROWS):
            s = pl.ds(i, ROWS)
            update = [[0.0, 0.0], [0.0, 0.0]]
            cosine, sine = lane_tw[0, :1, :], lane_tw[1, :1, :]
            for k in range(2):
                parts = []
                for part in range(2):
                    at = pl.ds((2 * k + part) * EDGE + i, ROWS)
                    parts.append(dot(cat([xh[at, :], xl[at, :], xh[at, :]], 1), left_hhl))
                ar, ai = parts[0][:, :HALF], parts[0][:, HALF:]
                br, bi = parts[1][:, :HALF], parts[1][:, HALF:]
                br, bi = br * cosine - bi * sine, bi * cosine + br * sine
                for h, real, imag in ((0, ar + br, ai + bi), (1, ar - br, ai - bi)):
                    cols = pl.ds(h * HALF, HALF)
                    pr, pi = probe[0, k, s, cols], probe[1, k, s, cols]
                    update[0][h] += pr * real + pi * imag
                    update[1][h] += pr * imag - pi * real
                    vr, vi = patch[0, s, cols], patch[1, s, cols]
                    sums[k, s, cols] += vr * real + vi * imag
                    sums[2 + k, s, cols] += vr * imag - vi * real
                    if k == 0:
                        sums[4, s, cols] += vr * vr + vi * vi
            for plane in range(2):
                for b, block in enumerate(spread(*update[plane], down, shift)):
                    at = (plane, pl.ds(first + i, ROWS + 8), pl.ds(base + b * HALF, HALF))
                    grad[at] += block
        return 0

    lax.fori_loop(0, metas[4, 0, 2 * SLOTS], visit, 0)


def tile_terms(place, metas, framed, probe, amps):
    vmem = pl.BlockSpec(memory_space=pltpu.VMEM)
    smem = pl.BlockSpec(memory_space=pltpu.SMEM)
    f32, bf16 = jnp.float32, jnp.bfloat16
    consts = tables()
    return pl.pallas_call(
        tile_kernel,
        out_shape=(
            jax.ShapeDtypeStruct((2, EXT, EXT), f32),
            jax.ShapeDtypeStruct((TILE, TILE), f32),
            jax.ShapeDtypeStruct((5, EDGE, EDGE), f32),
        ),
        in_specs=[smem, smem] + [vmem] * (3 + len(consts)),
        out_specs=(vmem, vmem, vmem),
        scratch_shapes=[
            pltpu.VMEM((2, EDGE, EDGE), f32),
            pltpu.VMEM((4 * EDGE, EDGE), bf16),
            pltpu.VMEM((4 * EDGE, EDGE), bf16),
            pltpu.VMEM((4, EDGE, EDGE), bf16),
            pltpu.VMEM((4, EDGE, EDGE), bf16),
            pltpu.VMEM((EDGE, EDGE), f32),
            pltpu.VMEM((LIT, LIT_PAD), f32),
            pltpu.VMEM((EDGE, EDGE), f32),
        ],
        compiler_params=pltpu.CompilerParams(vmem_limit_bytes=56 * 1024 * 1024),
        name="tile",
    )(place, metas, framed, probe, amps, *consts)


def on_device(field, probe, offsets, counts, amps):
    row, col = lax.axis_index("row"), lax.axis_index("col")
    meta = jnp.concatenate([offsets.reshape(2 * SLOTS), counts.reshape(1)])
    meta = jnp.broadcast_to(jnp.pad(meta, (0, 128 - 2 * SLOTS - 1))[None], (8, 128))
    framed, metas = gather_frame(field, meta)
    place = jnp.stack([row * TILE, col * TILE]).astype(jnp.int32)
    grad, shade, sums = tile_terms(place, metas, framed, probe, amps[0, 0])
    return finish(field, probe, grad, shade, sums)


def finish(field, probe, grad, shade, sums):
    inner = grad
    for axis, dim in (("row", 1), ("col", 2)):
        count = lax.axis_size(axis)
        size = inner.shape[dim]
        head = lax.slice_in_dim(inner, 0, MARGIN, axis=dim)
        tail = lax.slice_in_dim(inner, size - MARGIN, size, axis=dim)
        body = lax.slice_in_dim(inner, MARGIN, size - MARGIN, axis=dim)
        from_prev = lax.ppermute(tail, axis, [(i, (i + 1) % count) for i in range(count)])
        from_next = lax.ppermute(head, axis, [((i + 1) % count, i) for i in range(count)])
        pad = [[0, 0], [0, 0], [0, 0]]
        pad[dim] = [0, TILE - MARGIN]
        low = jnp.pad(from_prev, pad)
        pad[dim] = [TILE - MARGIN, 0]
        inner = body + low + jnp.pad(from_next, pad)
    total = lax.psum(sums, ("row", "col"))
    probe_new = probe + total[:4].reshape(2, 2, EDGE, EDGE) / (total[4] + 1.0)
    return (field + inner * shade[None], probe_new)


def solution(mesh):
    in_specs = (
        P(None, "row", "col"),
        P(),
        P("row", "col", None, None),
        P("row", "col"),
        P("row", "col", None, None, None),
    )
    out_specs = (P(None, "row", "col"), P())
    return jax.shard_map(
        on_device, mesh=mesh, in_specs=in_specs, out_specs=out_specs, check_vma=False
    )
```

time: 617 us -> 379 us (0.61)
  waiting for transfers between devices: 396 us -> 266 us
  Pallas kernels: 0 us -> 76.7 us
  starting transfers between devices: 66.3 us -> 8.08 us
  other arithmetic: 57.7 us -> 5.9 us
  local copies, waits for them, and re-layouts: 58.4 us -> 6.72 us
  matrix products: 14.7 us -> 0 us
    psum x1, waiting for transfers between devices: 349 us -> 252 us  [finish(): total = lax.psum(sums, ('row', 'col'))]
    pallas_call x0 -> x2, Pallas kernels: none -> 76.7 us  [the longest x1 42 us: gather_frame(): pl.pallas_call(halo_kernel, out_shape=(jax.ShapeDtypeStruct((2, EXT, EXT)...]
    ppermute x8 -> x4, starting transfers between devices: 66.2 us -> 8.05 us  [the longest x2 6.5 us: finish(): lax.ppermute(head, axis, [((i + 1) % count, i) for i in range(count)])]
    ppermute x8 -> x4, waiting for transfers between devices: 47.3 us -> 13.4 us  [the longest x2 9.51 us: finish(): lax.ppermute(tail, axis, [(i, (i + 1) % count) for i in range(count)])]
    dynamic_update_slice x6 -> x0, local copies, waits for them, and re-layouts: 21.4 us -> none  [add_window(): lax.dynamic_update_slice(canvas, window + values, (0, row_start, col_start))]
    dot_general x8 -> x0, matrix products: 14.7 us -> none  [the longest x4 7.37 us: transform(): jnp.einsum('jk,bji->bki', table_pair, stacked, precision=HIGHEST)]
    add x13 -> x4, other arithmetic: 17.4 us -> 5.22 us  [the longest x1 2.27 us: finish(): inner = body + low + jnp.pad(from_next, pad)]
    reduce_sum x5 -> x0, other arithmetic: 9.79 us -> none  [the longest x2 5.92 us: slot_terms(): jnp.sum(probe_real * back_real + probe_imag * back_imag, axis=0)]
  transfers between devices with their start and end apart: 9 -> 5, of which waited for: 7 -> 3; matrix products, arithmetic and copies ran while one was open for 3% -> 0% of each run, Pallas kernels for 0% -> 0%
where the time goes in v1:
time: 379 us; the launch traced here: 378 us
  waiting for transfers between devices  266 us (70%)
  Pallas kernels  76.7 us (20%)
  between operations  14.8 us (4%)
  starting transfers between devices  8.08 us (2%)
  local copies, waits for them, and re-layouts  6.72 us (2%)
  other arithmetic  5.9 us (2%)
    psum x1, waiting for transfers between devices, finish(): total = lax.psum(sums, ('row', 'col'))  252 us
    pallas_call x1, Pallas kernels, gather_frame(): pl.pallas_call(halo_kernel, out_shape=(jax.ShapeDtypeStruct((2, EXT, EXT)...  42 us
    pallas_call x1, Pallas kernels, tile_terms(): pl.pallas_call(tile_kernel, out_shape=(jax.ShapeDtypeStruct((2, EXT, EXT)...  34.7 us
    ppermute x2, waiting for transfers between devices, finish(): lax.ppermute(tail, axis, [(i, (i + 1) % count) for i in range(count)])  9.51 us
  transfers between devices with their start and end apart: 5, of which 3 were waited for; matrix products, arithmetic and copies ran while one was open for 0% of the time, Pallas kernels for 0%

profile of v1, /device:TPU:1, one launch (start us, length us, event | category | flops | bytes accessed | tf_op | source)
XLA Modules:
  0.0 377.8 jit_solution(10284159591128482155)
XLA Ops:
  7.2 0.0 all-reduce.7.cloned.1.call-start
  7.9 0.8 reshape.22
  8.6 0.6 pad_add_fusion.1.place
  9.2 0.1 pad_add_fusion.2
  9.3 0.0 copy-start
  9.3 1.6 copy-done
  10.9 42.0 %halo.1 = (f32[2,768,768]{2,1,0:T(8,128)S(1)}, s32[9,8,128]{2,1,0:T(8,128)S(1)}) custom-call(f32[2,512,512]{2,1,0:T(8,128)S(1)} %copy-done, s32[8,128]{1,0:T(8,128)S(1)} %broadcast_in_dim.2.meta), custom_call_target="tpu_custom_call" | custom-call | tf_op jit(solution)/shard_map/halo/pallas_call | solution.py:87
  52.9 0.0 copy-start.2
  52.9 2.2 copy-done.2
  55.1 0.0 copy-start.3
  55.1 0.6 copy-done.3
  55.7 34.7 %tile.1 = (f32[2,768,768]{2,1,0:T(8,128)}, f32[512,512]{1,0:T(8,128)}, f32[5,256,256]{2,1,0:T(8,128)}) custom-call(s32[2]{0:T(128)} %pad_add_fusion.1.place, s32[9,8,128]{2,1,0:T(8,128)} %copy-done.3, f32[2,768,768]{2,1,0:T(8,128)} %copy-done.2, f32[2,2,256,256]{3,2,1,0:T(8,128)} %probe.1, bf16[6,256,256]{2,1,0:T(8,128)(2,1)} %bitcast.9, ...), custom_call_target="tpu_custom_call" | custom-call | tf_op jit(solution)/shard_map/tile/pallas_call | solution.py:356
  90.4 1.5 fusion.4
  91.9 0.1 collective-permute-start
  92.0 5.7 %collective-permute-start.1 = (f32[2,128,768]{2,1,0:T(8,128)S(1)}, f32[2,128,768]{2,1,0:T(8,128)S(1)}, u32[]{:S(2)}, u32[]{:S(2)}) collective-permute-start(f32[2,128,768]{2,1,0:T(8,128)S(1)} %get-tuple-element.13), channel_id=1, source_target_pairs={{8,0},{16,8},{24,16},{32,24},{40,32},{48,40},{56,48},{64,56},{72,6... | collective-permute-start | bytes 2359304 | tf_op jit(solution)/shard_map/ppermute | solution.py:399
  97.7 0.0 all-reduce.7.cloned.1.call-update
  97.7 252.2 %all-reduce.7.cloned.1.call-done = f32[5,256,256]{2,1,0:T(8,128)} async-done(((f32[5,256,256]{2,1,0:T(8,128)}), f32[5,256,256]{2,1,0:T(8,128)}) %all-reduce.7.cloned.1.call-update) | async-done | bytes 1310736 | tf_op jit(solution)/shard_map/psum | solution.py:405
  349.9 0.0 collective-permute-done
  349.9 0.0 collective-permute-done.1
  349.9 0.0 copy-start.5
  349.9 2.3 pad_add_fusion
  352.2 0.0 copy-start.4
  352.2 0.0 slice-start
  352.2 0.1 fusion.5
  352.3 0.0 copy-start.1
  352.3 0.0 copy-start.6
  352.3 1.5 collective-permute-start.2
  353.8 0.8 collective-permute-start.3
  354.6 0.0 copy-done.4
  354.6 0.0 copy-done.5
  354.6 0.0 slice-done
  354.6 1.1 divide_add_fusion
  355.8 9.5 %collective-permute-done.2 = f32[2,512,128]{2,1,0:T(8,128)S(1)} collective-permute-done((f32[2,512,128]{2,1,0:T(8,128)S(1)}, f32[2,512,128]{2,1,0:T(8,128)S(1)}, u32[]{:S(2)}, u32[]{:S(2)}) %collective-permute-start.2) | collective-permute-done | bytes 524320 | tf_op jit(solution)/shard_map/ppermute | solution.py:398
  365.3 3.9 %collective-permute-done.3 = f32[2,512,128]{2,1,0:T(8,128)S(1)} collective-permute-done((f32[2,512,128]{2,1,0:T(8,128)S(1)}, f32[2,512,128]{2,1,0:T(8,128)S(1)}, u32[]{:S(2)}, u32[]{:S(2)}) %collective-permute-start.3) | collective-permute-done | bytes 524320 | tf_op jit(solution)/shard_map/ppermute | solution.py:399
  369.2 0.0 copy-done.1
  369.2 0.0 copy-done.6
  369.2 1.8 fusion.2
  (3 shorter events, 0.0 us)
Async XLA Ops:
  7.2 342.7 %all-reduce.7.cloned.1.call-start = ((), (), s32[]{:S(2)}) async-start(), calls=%async_computation | async-start | bytes 2621440 | tf_op jit(solution)/shard_map/psum | solution.py:405
  9.3 1.6 copy-start
  52.9 2.2 copy-start.2
  55.1 0.6 copy-start.3
  91.9 258.0 %collective-permute-start = (f32[2,128,768]{2,1,0:T(8,128)S(1)}, f32[2,128,768]{2,1,0:T(8,128)S(1)}, u32[]{:S(2)}, u32[]{:S(2)}) collective-permute-start(f32[2,128,768]{2,1,0:T(8,128)S(1)} %get-tuple-element.12), channel_id=1, source_target_pairs={{0,8},{8,16},{16,24},{24,32},{32,40},{40,48},{48,56},{56,64},{64,7... | collective-permute-start | bytes 2359304 | tf_op jit(solution)/shard_map/ppermute | solution.py:398
  92.0 257.9 %collective-permute-start.1 = (f32[2,128,768]{2,1,0:T(8,128)S(1)}, f32[2,128,768]{2,1,0:T(8,128)S(1)}, u32[]{:S(2)}, u32[]{:S(2)}) collective-permute-start(f32[2,128,768]{2,1,0:T(8,128)S(1)} %get-tuple-element.13), channel_id=1, source_target_pairs={{8,0},{16,8},{24,16},{32,24},{40,32},{48,40},{56,48},{64,56},{72,6... | collective-permute-start | bytes 2359304 | tf_op jit(solution)/shard_map/ppermute | solution.py:399
  349.9 4.7 %copy-start.5 = (f32[2,2,256,256]{3,2,1,0:T(8,128)S(1)}, f32[2,2,256,256]{3,2,1,0:T(8,128)}, u32[]{:S(2)}) copy-start(f32[2,2,256,256]{3,2,1,0:T(8,128)} %probe.1) | copy-start | bytes 3145732
  352.2 2.4 copy-start.4
  352.2 2.4 slice-start
  352.3 16.9 %copy-start.1 = (f32[2,512,512]{2,1,0:T(8,128)S(1)}, f32[2,512,512]{2,1,0:T(8,128)}, u32[]{:S(2)}) copy-start(f32[2,512,512]{2,1,0:T(8,128)} %field.1) | copy-start | bytes 6291460
  352.3 16.9 %copy-start.6 = (f32[512,512]{1,0:T(8,128)S(1)}, f32[512,512]{1,0:T(8,128)}, u32[]{:S(2)}) copy-start(f32[512,512]{1,0:T(8,128)} %get-tuple-element.10) | copy-start | bytes 3145732
  352.3 13.0 %collective-permute-start.2 = (f32[2,512,128]{2,1,0:T(8,128)S(1)}, f32[2,512,128]{2,1,0:T(8,128)S(1)}, u32[]{:S(2)}, u32[]{:S(2)}) collective-permute-start(f32[2,512,128]{2,1,0:T(8,128)S(1)} %get-tuple-element.14), channel_id=1, source_target_pairs={{0,1},{1,2},{2,3},{3,4},{4,5},{5,6},{6,7},{7,0},{8,9},{9,10},{10,1... | collective-permute-start | bytes 1572872 | tf_op jit(solution)/shard_map/ppermute | solution.py:398
  353.8 15.4 %collective-permute-start.3 = (f32[2,512,128]{2,1,0:T(8,128)S(1)}, f32[2,512,128]{2,1,0:T(8,128)S(1)}, u32[]{:S(2)}, u32[]{:S(2)}) collective-permute-start(f32[2,512,128]{2,1,0:T(8,128)S(1)} %get-tuple-element.15), channel_id=1, source_target_pairs={{1,0},{2,1},{3,2},{4,3},{5,4},{6,5},{7,6},{0,7},{9,8},{10,9},{11,1... | collective-permute-start | bytes 1572872 | tf_op jit(solution)/shard_map/ppermute | solution.py:399
Sparse Core Ops, SparseCore 0:
  97.8 252.0 all-reduce.6

commit v2 on v1

--- a/solution.py
+++ b/solution.py
@@ -377,6 +377,197 @@
     )(place, metas, framed, probe, amps, *consts)
 
 
+RIM_SOURCE = {-1: (0, MARGIN), 0: (MARGIN, TILE), 1: (MARGIN + TILE, MARGIN)}
+RIM_TARGET = {1: (0, MARGIN), 0: (0, TILE), -1: (TILE - MARGIN, MARGIN)}
+
+
+def torus_place():
+    row, col = lax.axis_index("row"), lax.axis_index("col")
+    return (
+        row // 8,
+        lax.rem(row, 4),
+        (col // 2) * 2 + lax.rem(row // 4, 2),
+        lax.rem(col, 2),
+    )
+
+
+def torus_device(x, y, z, core):
+    return (x * 8 + lax.rem(z, 2) * 4 + y, (z // 2) * 2 + core)
+
+
+def fold_kernel(
+    grad, field, shade, sums, probe, object_out, probe_out,
+    inner, base, lit, rims_r, rims_c, rims_d, pair_in, x_in, y_in, z_in, acc, rows_out, row_new, rows_in, spread,
+    local_sems, rim_send, rim_recv, red_send, red_recv, put_send, put_recv,
+):
+    f32 = jnp.float32
+    x, y, z, core = torus_place()
+    pair = torus_device(x, y, z, 1 - core)
+    x_peers = [torus_device(lax.rem(x + d, 4), y, z, core) for d in range(1, 4)]
+    y_peers = [torus_device(x, lax.rem(y + d, 4), z, core) for d in range(1, 4)]
+    z_peers = [torus_device(x, y, lax.rem(z + d, 8), core) for d in range(1, 8)]
+
+    def ref_of(n):
+        if n < 2:
+            return rims_c.at[n]
+        if n < 6:
+            return rims_d.at[n - 2]
+        return rims_r.at[n - 6]
+
+    barrier = pltpu.get_barrier_semaphore()
+    partners = [shifted(dr, dc) for dr, dc in NEIGHBOURS] + [pair] + x_peers + y_peers + z_peers
+    for device in partners:
+        pl.semaphore_signal(barrier, inc=1, device_id=device, device_id_type=MESH)
+    locals_ = [
+        pltpu.make_async_copy(
+            grad.at[:, pl.ds(MARGIN, TILE), pl.ds(MARGIN, TILE)], inner, local_sems.at[0]
+        ),
+        pltpu.make_async_copy(field, base, local_sems.at[1]),
+        pltpu.make_async_copy(shade, lit, local_sems.at[2]),
+    ]
+    pl.semaphore_wait(barrier, len(partners))
+
+    def send(src, dst, device, sems, n):
+        copy = pltpu.make_async_remote_copy(
+            src_ref=src,
+            dst_ref=dst,
+            send_sem=sems[0].at[n],
+            recv_sem=sems[1].at[n],
+            device_id=device,
+            device_id_type=MESH,
+        )
+        copy.start()
+        return copy
+
+    red, put = (red_send, red_recv), (put_send, put_recv)
+    half = pl.multiple_of(core * HALF, HALF)
+    other = pl.multiple_of((1 - core) * HALF, HALF)
+    to_pair = send(sums.at[:, pl.ds(other, HALF), :], pair_in, pair, red, 0)
+    rims = []
+    for n, (dr, dc) in enumerate(NEIGHBOURS):
+        src = grad.at[:, pl.ds(*RIM_SOURCE[dr]), pl.ds(*RIM_SOURCE[dc])]
+        rims.append(send(src, ref_of(n), shifted(dr, dc), (rim_send, rim_recv), n))
+    for copy in locals_:
+        copy.start()
+
+    to_pair.wait()
+    for i in range(0, HALF, ROWS):
+        rows = pl.ds(i, ROWS)
+        acc[:, rows, :] = sums[:, pl.ds(pl.multiple_of(half + i, ROWS), ROWS), :] + pair_in[:, rows, :]
+    copies = []
+    for d in range(1, 4):
+        at = pl.multiple_of(lax.rem(x + d, 4) * 32, 32)
+        copies.append(send(acc.at[:, pl.ds(at, 32), :], x_in.at[d - 1], x_peers[d - 1], red, d))
+    for copy in copies:
+        copy.wait()
+    x_at = pl.multiple_of(x * 32, 32)
+    mine = acc[:, pl.ds(x_at, 32), :]
+    for d in range(3):
+        mine = mine + x_in[d]
+    acc[:, pl.ds(x_at, 32), :] = mine
+    copies = []
+    for d in range(1, 4):
+        at = pl.multiple_of(x_at + lax.rem(y + d, 4) * 8, 8)
+        copies.append(send(acc.at[:, pl.ds(at, 8), :], y_in.at[d - 1], y_peers[d - 1], red, 3 + d))
+    for copy in copies:
+        copy.wait()
+    y_at = pl.multiple_of(x_at + y * 8, 8)
+    mine = acc[:, pl.ds(y_at, 8), :]
+    for d in range(3):
+        mine = mine + y_in[d]
+    rows_out[...] = jnp.zeros_like(rows_out)
+    for r in range(8):
+        for p in range(5):
+            rows_out[r, pl.ds(p, 1), :] = mine[p, r : r + 1, :]
+    copies = []
+    for d in range(1, 8):
+        copies.append(send(rows_out.at[lax.rem(z + d, 8)], z_in.at[d - 1], z_peers[d - 1], red, 6 + d))
+    for copy in copies:
+        copy.wait()
+    total = rows_out[z]
+    for d in range(7):
+        total = total + z_in[d]
+    row_new[...] = total / (total[4:5] + 1.0)
+
+    copies = []
+    for d in range(1, 8):
+        copies.append(send(row_new, rows_in.at[z], z_peers[d - 1], put, d))
+    rows_in[z] = row_new[...]
+    for copy in copies:
+        copy.wait()
+    at = pl.multiple_of(half + y_at, 8)
+    for p in range(4):
+        spread[p, pl.ds(at, 8), :] = jnp.concatenate([rows_in[r, pl.ds(p, 1), :] for r in range(8)], 0)
+    copies = []
+    block = spread.at[:, pl.ds(at, 8), :]
+    for d in range(1, 4):
+        copies.append(send(block, block, y_peers[d - 1], put, 7 + d))
+    for copy in copies:
+        copy.wait()
+    block = spread.at[:, pl.ds(pl.multiple_of(half + x_at, 32), 32), :]
+    copies = []
+    for d in range(1, 4):
+        copies.append(send(block, block, x_peers[d - 1], put, 10 + d))
+    for copy in copies:
+        copy.wait()
+    block = spread.at[:, pl.ds(half, HALF), :]
+    last = send(block, block, pair, put, 0)
+
+    for copy in locals_:
+        copy.wait()
+    for n, (dr, dc) in enumerate(NEIGHBOURS):
+        rims[n].wait()
+        (r0, rn), (c0, cn) = RIM_TARGET[dr], RIM_TARGET[dc]
+        for i in range(0, rn, 64):
+            inner[:, pl.ds(r0 + i, 64), pl.ds(c0, cn)] += ref_of(n)[:, pl.ds(i, 64), :]
+    for i in range(0, TILE, ROWS):
+        rows = pl.ds(i, ROWS)
+        for c in range(2):
+            object_out[c, rows, :] = base[c, rows, :] + inner[c, rows, :] * lit[rows, :]
+    last.wait()
+    for c in range(2):
+        for k in range(2):
+            probe_out[c, k] = probe[c, k] + spread[2 * c + k]
+
+
+def fold(grad, field, shade, sums, probe):
+    vmem = pl.BlockSpec(memory_space=pltpu.VMEM)
+    any_spec = pl.BlockSpec(memory_space=pl.ANY)
+    f32 = jnp.float32
+    dma = pltpu.SemaphoreType.DMA
+    return pl.pallas_call(
+        fold_kernel,
+        out_shape=(
+            jax.ShapeDtypeStruct((2, TILE, TILE), f32),
+            jax.ShapeDtypeStruct((2, 2, EDGE, EDGE), f32),
+        ),
+        in_specs=[any_spec, any_spec, any_spec, vmem, vmem],
+        out_specs=(vmem, vmem),
+        scratch_shapes=[
+            pltpu.VMEM((2, TILE, TILE), f32),
+            pltpu.VMEM((2, TILE, TILE), f32),
+            pltpu.VMEM((TILE, TILE), f32),
+            pltpu.VMEM((2, 2, MARGIN, TILE), f32),
+            pltpu.VMEM((2, 2, TILE, MARGIN), f32),
+            pltpu.VMEM((4, 2, MARGIN, MARGIN), f32),
+            pltpu.VMEM((5, HALF, EDGE), f32),
+            pltpu.VMEM((3, 5, 32, EDGE), f32),
+            pltpu.VMEM((3, 5, 8, EDGE), f32),
+            pltpu.VMEM((7, 8, EDGE), f32),
+            pltpu.VMEM((5, HALF, EDGE), f32),
+            pltpu.VMEM((8, 8, EDGE), f32),
+            pltpu.VMEM((8, EDGE), f32),
+            pltpu.VMEM((8, 8, EDGE), f32),
+            pltpu.VMEM((4, EDGE, EDGE), f32),
+            dma((3,)), dma((8,)), dma((8,)), dma((14,)), dma((14,)), dma((14,)), dma((14,)),
+        ],
+        compiler_params=pltpu.CompilerParams(
+            collective_id=1, has_side_effects=True, vmem_limit_bytes=40 * 1024 * 1024
+        ),
+        name="fold",
+    )(grad, field, shade, sums, probe)
+
+
 def on_device(field, probe, offsets, counts, amps):
     row, col = lax.axis_index("row"), lax.axis_index("col")
     meta = jnp.concatenate([offsets.reshape(2 * SLOTS), counts.reshape(1)])
@@ -384,27 +575,7 @@
     framed, metas = gather_frame(field, meta)
     place = jnp.stack([row * TILE, col * TILE]).astype(jnp.int32)
     grad, shade, sums = tile_terms(place, metas, framed, probe, amps[0, 0])
-    return finish(field, probe, grad, shade, sums)
-
-
-def finish(field, probe, grad, shade, sums):
-    inner = grad
-    for axis, dim in (("row", 1), ("col", 2)):
-        count = lax.axis_size(axis)
-        size = inner.shape[dim]
-        head = lax.slice_in_dim(inner, 0, MARGIN, axis=dim)
-        tail = lax.slice_in_dim(inner, size - MARGIN, size, axis=dim)
-        body = lax.slice_in_dim(inner, MARGIN, size - MARGIN, axis=dim)
-        from_prev = lax.ppermute(tail, axis, [(i, (i + 1) % count) for i in range(count)])
-        from_next = lax.ppermute(head, axis, [((i + 1) % count, i) for i in range(count)])
-        pad = [[0, 0], [0, 0], [0, 0]]
-        pad[dim] = [0, TILE - MARGIN]
-        low = jnp.pad(from_prev, pad)
-        pad[dim] = [TILE - MARGIN, 0]
-        inner = body + low + jnp.pad(from_next, pad)
-    total = lax.psum(sums, ("row", "col"))
-    probe_new = probe + total[:4].reshape(2, 2, EDGE, EDGE) / (total[4] + 1.0)
-    return (field + inner * shade[None], probe_new)
+    return fold(grad, field, shade, sums, probe)
 
 
 def solution(mesh):

time: 379 us -> 150 us (0.40)
  waiting for transfers between devices: 266 us -> 0 us
  Pallas kernels: 76.7 us -> 136 us
  between operations: 14.8 us -> 1.33 us
  starting transfers between devices: 8.08 us -> 0 us
  local copies, waits for them, and re-layouts: 6.72 us -> 12.3 us
  other arithmetic: 5.9 us -> 0.71 us
    psum x1 -> x0, waiting for transfers between devices: 252 us -> none  [finish(): total = lax.psum(sums, ('row', 'col'))]
    pallas_call x0 -> x1, Pallas kernels: none -> 80.7 us  [fold(): pl.pallas_call(fold_kernel, out_shape=(jax.ShapeDtypeStruct((2, TILE, TIL...]
    pallas_call x1, Pallas kernels: 34.7 us -> 12.9 us  [tile_terms(): pl.pallas_call(tile_kernel, out_shape=(jax.ShapeDtypeStruct((2, EXT, EXT)...]
    ppermute x4 -> x0, waiting for transfers between devices: 13.4 us -> none  [the longest x2 9.51 us: finish(): lax.ppermute(tail, axis, [(i, (i + 1) % count) for i in range(count)])]
    ppermute x4 -> x0, starting transfers between devices: 8.05 us -> none  [the longest x2 6.5 us: finish(): lax.ppermute(head, axis, [((i + 1) % count, i) for i in range(count)])]
    unnamed x14 -> x18, local copies, waits for them, and re-layouts: 4.39 us -> 11.5 us
    add x4 -> x0, other arithmetic: 5.22 us -> none  [the longest x1 2.27 us: finish(): inner = body + low + jnp.pad(from_next, pad)]
  transfers between devices with their start and end apart: 5 -> 0, of which waited for: 3 -> 0; matrix products, arithmetic and copies ran while one was open for 0% -> 0% of each run, Pallas kernels for 0% -> 0%
where the time goes in v2:
time: 150 us
  Pallas kernels  136 us (91%)
  local copies, waits for them, and re-layouts  12.3 us (8%)
    pallas_call x1, Pallas kernels, fold(): pl.pallas_call(fold_kernel, out_shape=(jax.ShapeDtypeStruct((2, TILE, TIL...  80.7 us
    pallas_call x1, Pallas kernels, gather_frame(): pl.pallas_call(halo_kernel, out_shape=(jax.ShapeDtypeStruct((2, EXT, EXT)...  42 us
    pallas_call x1, Pallas kernels, tile_terms(): pl.pallas_call(tile_kernel, out_shape=(jax.ShapeDtypeStruct((2, EXT, EXT)...  12.9 us
    unnamed x18, local copies, waits for them, and re-layouts  11.5 us

profile of v2, /device:TPU:1, one launch (start us, length us, event | category | flops | bytes accessed | tf_op | source)
XLA Modules:
  0.0 149.9 jit_solution(1828778680495280011)
XLA Ops:
  1.3 0.6 pad_add_fusion.place
  1.9 0.8 reshape.11
  2.7 0.1 pad_add_fusion.1
  2.8 0.0 copy-start
  2.8 1.6 %copy-done = f32[2,512,512]{2,1,0:T(8,128)S(1)} copy-done((f32[2,512,512]{2,1,0:T(8,128)S(1)}, f32[2,512,512]{2,1,0:T(8,128)}, u32[]{:S(2)}) %copy-start) | copy-done | bytes 2097176
  4.4 42.0 %halo.1 = (f32[2,768,768]{2,1,0:T(8,128)S(1)}, s32[9,8,128]{2,1,0:T(8,128)S(1)}) custom-call(f32[2,512,512]{2,1,0:T(8,128)S(1)} %copy-done, s32[8,128]{1,0:T(8,128)S(1)} %broadcast_in_dim.2.meta), custom_call_target="tpu_custom_call" | custom-call | tf_op jit(solution)/shard_map/halo/pallas_call | solution.py:87
  46.4 0.0 copy-start.3
  46.4 2.1 %copy-done.3 = f32[2,768,768]{2,1,0:T(8,128)} copy-done((f32[2,768,768]{2,1,0:T(8,128)}, f32[2,768,768]{2,1,0:T(8,128)S(1)}, u32[]{:S(2)}) %copy-start.3) | copy-done | bytes 4718616
  48.5 0.0 copy-start.7
  48.5 0.6 copy-done.7
  49.1 0.0 copy-start.1
  49.1 0.0 copy-start.4
  49.1 12.9 %tile.1 = (f32[2,768,768]{2,1,0:T(8,128)}, f32[512,512]{1,0:T(8,128)}, f32[5,256,256]{2,1,0:T(8,128)}) custom-call(s32[2]{0:T(128)} %pad_add_fusion.place, s32[9,8,128]{2,1,0:T(8,128)} %copy-done.7, f32[2,768,768]{2,1,0:T(8,128)} %copy-done.3, f32[2,2,256,256]{3,2,1,0:T(8,128)} %probe.3, bf16[6,256,256]{2,1,0:T(8,128)(2,1)} %bitcast.5, ...), custom_call_target="tpu_custom_call" | custom-call | tf_op jit(solution)/shard_map/tile/pallas_call | solution.py:356
  62.0 0.0 copy-done.1
  62.0 0.0 copy-done.4
  62.0 0.0 copy-start.2
  62.0 2.3 %copy-done.2 = f32[2,768,768]{2,1,0:T(8,128)S(1)} copy-done((f32[2,768,768]{2,1,0:T(8,128)S(1)}, f32[2,768,768]{2,1,0:T(8,128)}, u32[]{:S(2)}) %copy-start.2) | copy-done | bytes 4718616
  64.4 0.0 copy-start.5
  64.4 1.3 copy-done.5
  65.7 0.0 copy-start.6
  65.7 1.2 copy-done.6
  66.9 80.7 %fold.1 = (f32[2,512,512]{2,1,0:T(8,128)S(1)}, f32[2,2,256,256]{3,2,1,0:T(8,128)S(1)}) custom-call(f32[2,768,768]{2,1,0:T(8,128)S(1)} %copy-done.2, f32[2,512,512]{2,1,0:T(8,128)S(1)} %copy-done.1, f32[512,512]{1,0:T(8,128)S(1)} %copy-done.6, f32[5,256,256]{2,1,0:T(8,128)S(1)} %copy-done.5, f32[2,2,256,256]{3,2,1,0:T(8,128)S(1)} %copy-done.4), custom_call_target="tpu_custom_call" | custom-call | tf_op jit(solution)/shard_map/fold/pallas_call | solution.py:538
  147.6 1.3 copy.18
  148.9 1.0 copy.19
  (2 shorter events, 0.0 us)
Async XLA Ops:
  2.8 1.6 %copy-start = (f32[2,512,512]{2,1,0:T(8,128)S(1)}, f32[2,512,512]{2,1,0:T(8,128)}, u32[]{:S(2)}) copy-start(f32[2,512,512]{2,1,0:T(8,128)} %field.3) | copy-start | bytes 6291460
  46.4 2.1 %copy-start.3 = (f32[2,768,768]{2,1,0:T(8,128)}, f32[2,768,768]{2,1,0:T(8,128)S(1)}, u32[]{:S(2)}) copy-start(f32[2,768,768]{2,1,0:T(8,128)S(1)} %get-tuple-element.8.framed) | copy-start | bytes 14155780
  48.5 0.6 copy-start.7
  49.1 12.9 %copy-start.1 = (f32[2,512,512]{2,1,0:T(8,128)S(1)}, f32[2,512,512]{2,1,0:T(8,128)}, u32[]{:S(2)}) copy-start(f32[2,512,512]{2,1,0:T(8,128)} %field.3) | copy-start | bytes 6291460
  49.1 12.9 %copy-start.4 = (f32[2,2,256,256]{3,2,1,0:T(8,128)S(1)}, f32[2,2,256,256]{3,2,1,0:T(8,128)}, u32[]{:S(2)}) copy-start(f32[2,2,256,256]{3,2,1,0:T(8,128)} %probe.3) | copy-start | bytes 3145732
  62.0 2.3 %copy-start.2 = (f32[2,768,768]{2,1,0:T(8,128)S(1)}, f32[2,768,768]{2,1,0:T(8,128)}, u32[]{:S(2)}) copy-start(f32[2,768,768]{2,1,0:T(8,128)} %get-tuple-element.9.grad) | copy-start | bytes 14155780
  64.4 1.3 copy-start.5
  65.7 1.2 copy-start.6

commit v3 on v2

--- a/solution.py
+++ b/solution.py
@@ -84,6 +84,7 @@
 def gather_frame(field, meta):
     any_spec = pl.BlockSpec(memory_space=pl.ANY)
     count = len(NEIGHBOURS)
+    vmem = pl.BlockSpec(memory_space=pltpu.VMEM)
     return pl.pallas_call(
         halo_kernel,
         out_shape=(
@@ -91,7 +92,7 @@
             jax.ShapeDtypeStruct((9, 8, 128), jnp.int32),
         ),
         in_specs=[any_spec, any_spec],
-        out_specs=(any_spec, any_spec),
+        out_specs=(vmem, any_spec),
         scratch_shapes=[
             pltpu.SemaphoreType.DMA((2,)),
             pltpu.SemaphoreType.DMA((count,)),
@@ -100,7 +101,7 @@
             pltpu.SemaphoreType.DMA((count,)),
         ],
         compiler_params=pltpu.CompilerParams(
-            collective_id=0, has_side_effects=True, vmem_limit_bytes=4 * 1024 * 1024
+            collective_id=0, has_side_effects=True, vmem_limit_bytes=16 * 1024 * 1024
         ),
         name="halo",
     )(field, meta)
@@ -137,7 +138,7 @@
 def tile_kernel(
     place, metas, framed, probe, amps, rh, rl, lh, ll, pick, pick_t, lane_tw, sub_tw,
     grad, shade, sums,
-    patch, xh, xl, yh, yl, amp, light, power,
+    patch, xh, xl, yh, yl, amp, light, power, whole,
 ):
     f32, bf16 = jnp.float32, jnp.bfloat16
     dot = functools.partial(jnp.dot, preferred_element_type=f32)
@@ -247,14 +248,14 @@
                     xh[at, :] = high
                     xl[at, :] = low
 
+        whole[...] = dot(cat([xh[...], xl[...], xh[...]], 1), right_hhl)
         for k in range(2):
             for i in range(0, HALF, ROWS):
                 res = []
                 for row in (i, HALF + i):
-                    parts = []
-                    for part in range(2):
-                        at = pl.ds((2 * k + part) * EDGE + row, ROWS)
-                        parts.append(dot(cat([xh[at, :], xl[at, :], xh[at, :]], 1), right_hhl))
+                    parts = [
+                        whole[pl.ds((2 * k + part) * EDGE + row, ROWS), :] for part in range(2)
+                    ]
                     res.append(
                         (
                             cat([parts[0][:, :HALF], parts[1][:, :HALF]], 1),
@@ -317,15 +318,13 @@
                         xl[at, :] = low
 
         left_hhl = cat([lh[...], lh[...], ll[...]], 0)
+        whole[...] = dot(cat([xh[...], xl[...], xh[...]], 1), left_hhl)
         for i in range(0, EDGE, ROWS):
             s = pl.ds(i, ROWS)
             update = [[0.0, 0.0], [0.0, 0.0]]
             cosine, sine = lane_tw[0, :1, :], lane_tw[1, :1, :]
             for k in range(2):
-                parts = []
-                for part in range(2):
-                    at = pl.ds((2 * k + part) * EDGE + i, ROWS)
-                    parts.append(dot(cat([xh[at, :], xl[at, :], xh[at, :]], 1), left_hhl))
+                parts = [whole[pl.ds((2 * k + part) * EDGE + i, ROWS), :] for part in range(2)]
                 ar, ai = parts[0][:, :HALF], parts[0][:, HALF:]
                 br, bi = parts[1][:, :HALF], parts[1][:, HALF:]
                 br, bi = br * cosine - bi * sine, bi * cosine + br * sine
@@ -371,8 +370,9 @@
             pltpu.VMEM((EDGE, EDGE), f32),
             pltpu.VMEM((LIT, LIT_PAD), f32),
             pltpu.VMEM((EDGE, EDGE), f32),
+            pltpu.VMEM((4 * EDGE, EDGE), f32),
         ],
-        compiler_params=pltpu.CompilerParams(vmem_limit_bytes=56 * 1024 * 1024),
+        compiler_params=pltpu.CompilerParams(vmem_limit_bytes=40 * 1024 * 1024),
         name="tile",
     )(place, metas, framed, probe, amps, *consts)
 
@@ -397,7 +397,7 @@
 
 def fold_kernel(
     grad, field, shade, sums, probe, object_out, probe_out,
-    inner, base, lit, rims_r, rims_c, rims_d, pair_in, x_in, y_in, z_in, acc, rows_out, row_new, rows_in, spread,
+    base, rims_r, rims_c, rims_d, pair_in, x_in, y_in, z_in, acc, rows_out, row_new, rows_in, spread,
     local_sems, rim_send, rim_recv, red_send, red_recv, put_send, put_recv,
 ):
     f32 = jnp.float32
@@ -419,11 +419,7 @@
     for device in partners:
         pl.semaphore_signal(barrier, inc=1, device_id=device, device_id_type=MESH)
     locals_ = [
-        pltpu.make_async_copy(
-            grad.at[:, pl.ds(MARGIN, TILE), pl.ds(MARGIN, TILE)], inner, local_sems.at[0]
-        ),
-        pltpu.make_async_copy(field, base, local_sems.at[1]),
-        pltpu.make_async_copy(shade, lit, local_sems.at[2]),
+        pltpu.make_async_copy(field, base, local_sems.at[0]),
     ]
     pl.semaphore_wait(barrier, len(partners))
 
@@ -519,11 +515,15 @@
         rims[n].wait()
         (r0, rn), (c0, cn) = RIM_TARGET[dr], RIM_TARGET[dc]
         for i in range(0, rn, 64):
-            inner[:, pl.ds(r0 + i, 64), pl.ds(c0, cn)] += ref_of(n)[:, pl.ds(i, 64), :]
+            rows = pl.ds(r0 + i, 64)
+            base[:, rows, pl.ds(c0, cn)] += ref_of(n)[:, pl.ds(i, 64), :] * shade[rows, pl.ds(c0, cn)]
     for i in range(0, TILE, ROWS):
         rows = pl.ds(i, ROWS)
         for c in range(2):
-            object_out[c, rows, :] = base[c, rows, :] + inner[c, rows, :] * lit[rows, :]
+            object_out[c, rows, :] = (
+                base[c, rows, :]
+                + grad[c, pl.ds(MARGIN + i, ROWS), pl.ds(MARGIN, TILE)] * shade[rows, :]
+            )
     last.wait()
     for c in range(2):
         for k in range(2):
@@ -541,12 +541,10 @@
             jax.ShapeDtypeStruct((2, TILE, TILE), f32),
             jax.ShapeDtypeStruct((2, 2, EDGE, EDGE), f32),
         ),
-        in_specs=[any_spec, any_spec, any_spec, vmem, vmem],
+        in_specs=[vmem, any_spec, vmem, vmem, vmem],
         out_specs=(vmem, vmem),
         scratch_shapes=[
             pltpu.VMEM((2, TILE, TILE), f32),
-            pltpu.VMEM((2, TILE, TILE), f32),
-            pltpu.VMEM((TILE, TILE), f32),
             pltpu.VMEM((2, 2, MARGIN, TILE), f32),
             pltpu.VMEM((2, 2, TILE, MARGIN), f32),
             pltpu.VMEM((4, 2, MARGIN, MARGIN), f32),
@@ -559,10 +557,10 @@
             pltpu.VMEM((8, EDGE), f32),
             pltpu.VMEM((8, 8, EDGE), f32),
             pltpu.VMEM((4, EDGE, EDGE), f32),
-            dma((3,)), dma((8,)), dma((8,)), dma((14,)), dma((14,)), dma((14,)), dma((14,)),
+            dma((1,)), dma((8,)), dma((8,)), dma((14,)), dma((14,)), dma((14,)), dma((14,)),
         ],
         compiler_params=pltpu.CompilerParams(
-            collective_id=1, has_side_effects=True, vmem_limit_bytes=40 * 1024 * 1024
+            collective_id=1, has_side_effects=True, vmem_limit_bytes=32 * 1024 * 1024
         ),
         name="fold",
     )(grad, field, shade, sums, probe)

time: 150 us -> 134 us (0.89)
  Pallas kernels: 136 us -> 123 us
  local copies, waits for them, and re-layouts: 12.3 us -> 9.19 us
    pallas_call x1, Pallas kernels: 80.7 us -> 72.7 us  [fold(): pl.pallas_call(fold_kernel, out_shape=(jax.ShapeDtypeStruct((2, TILE, TIL...]
    pallas_call x1, Pallas kernels: 12.9 us -> 7.64 us  [tile_terms(): pl.pallas_call(tile_kernel, out_shape=(jax.ShapeDtypeStruct((2, EXT, EXT)...]
    unnamed x18 -> x26, local copies, waits for them, and re-layouts: 11.5 us -> 8.42 us
where the time goes in v3:
time: 134 us; the launch traced here: 133 us
  Pallas kernels  123 us (92%)
  local copies, waits for them, and re-layouts  9.19 us (7%)
  between operations  1.39 us (1%)
    pallas_call x1, Pallas kernels, fold(): pl.pallas_call(fold_kernel, out_shape=(jax.ShapeDtypeStruct((2, TILE, TIL...  72.7 us
    pallas_call x1, Pallas kernels, gather_frame(): pl.pallas_call(halo_kernel, out_shape=(jax.ShapeDtypeStruct((2, EXT, EXT)...  42.2 us
    unnamed x26, local copies, waits for them, and re-layouts  8.42 us
    pallas_call x1, Pallas kernels, tile_terms(): pl.pallas_call(tile_kernel, out_shape=(jax.ShapeDtypeStruct((2, EXT, EXT)...  7.64 us

profile of v3, /device:TPU:1, one launch (start us, length us, event | category | flops | bytes accessed | tf_op | source)
XLA Modules:
  0.0 133.3 jit_solution(12775733907184744109)
XLA Ops:
  0.6 0.0 copy-start.11
  1.3 0.1 pad_add_fusion.place
  1.4 0.8 reshape.11
  2.1 0.1 pad_add_fusion.1
  2.2 0.0 copy-start
  2.2 1.6 %copy-done = f32[2,512,512]{2,1,0:T(8,128)S(1)} copy-done((f32[2,512,512]{2,1,0:T(8,128)S(1)}, f32[2,512,512]{2,1,0:T(8,128)}, u32[]{:S(2)}) %copy-start) | copy-done | bytes 2097176
  3.8 0.0 copy-start.2
  3.8 0.0 copy-start.3
  3.8 0.0 copy-start.4
  3.8 0.0 copy-start.5
  3.8 42.2 %halo.1 = (f32[2,768,768]{2,1,0:T(8,128)S(1)}, s32[9,8,128]{2,1,0:T(8,128)S(1)}) custom-call(f32[2,512,512]{2,1,0:T(8,128)S(1)} %copy-done, s32[8,128]{1,0:T(8,128)S(1)} %broadcast_in_dim.2.meta), custom_call_target="tpu_custom_call" | custom-call | tf_op jit(solution)/shard_map/halo/pallas_call | solution.py:88
  46.0 0.0 copy-done.11
  46.0 0.0 copy-done.2
  46.0 0.0 copy-done.3
  46.1 0.0 copy-done.4
  46.1 0.0 copy-done.5
  46.1 0.0 copy-start.6
  46.1 0.9 copy-done.6
  47.0 0.0 copy-start.7
  47.0 0.9 copy-done.7
  47.9 0.0 copy-start.8
  47.9 0.9 copy-done.8
  48.8 0.0 copy-start.9
  48.8 0.9 copy-done.9
  49.7 0.0 copy-start.10
  49.7 0.9 copy-done.10
  50.6 0.0 copy-start.1
  50.6 7.6 %tile.1 = (f32[2,768,768]{2,1,0:T(8,128)S(1)}, f32[512,512]{1,0:T(8,128)S(1)}, f32[5,256,256]{2,1,0:T(8,128)S(1)}) custom-call(s32[2]{0:T(128)S(1)} %pad_add_fusion.place, s32[9,8,128]{2,1,0:T(8,128)S(1)} %get-tuple-element.7.metas, f32[2,768,768]{2,1,0:T(8,128)S(1)} %get-tuple-element.8.framed, f32[2,2,256,256]{3,2,1,0:T(8,128)S(1)} %copy-done.2, ...), custom_call_target="tpu_custom_call" | custom-call | tf_op jit(solution)/shard_map/tile/pallas_call | solution.py:355
  58.2 0.0 copy-done.1
  58.3 72.7 %fold.1 = (f32[2,512,512]{2,1,0:T(8,128)S(1)}, f32[2,2,256,256]{3,2,1,0:T(8,128)S(1)}) custom-call(f32[2,768,768]{2,1,0:T(8,128)S(1)} %get-tuple-element.9.grad, f32[2,512,512]{2,1,0:T(8,128)S(1)} %copy-done.1, f32[512,512]{1,0:T(8,128)S(1)} %get-tuple-element.10.shade, f32[5,256,256]{2,1,0:T(8,128)S(1)} %get-tuple-element.11.sums, ...), custom_call_target="tpu_custom_call" | custom-call | tf_op jit(solution)/shard_map/fold/pallas_call | solution.py:538
  131.0 1.3 copy.18
  132.3 1.0 copy.19
  (2 shorter events, 0.0 us)
Async XLA Ops:
  0.6 45.4 %copy-start.11 = (f32[2,8,128]{2,1,0:T(8,128)S(1)}, f32[2,8,128]{2,1,0:T(8,128)}, u32[]{:S(2)}) copy-start(f32[2,8,128]{2,1,0:T(8,128)} %constant.35.clone.lane_tw) | copy-start | bytes 24580
  2.2 1.6 %copy-start = (f32[2,512,512]{2,1,0:T(8,128)S(1)}, f32[2,512,512]{2,1,0:T(8,128)}, u32[]{:S(2)}) copy-start(f32[2,512,512]{2,1,0:T(8,128)} %field.3) | copy-start | bytes 6291460
  3.8 42.2 %copy-start.2 = (f32[2,2,256,256]{3,2,1,0:T(8,128)S(1)}, f32[2,2,256,256]{3,2,1,0:T(8,128)}, u32[]{:S(2)}) copy-start(f32[2,2,256,256]{3,2,1,0:T(8,128)} %probe.3) | copy-start | bytes 3145732
  3.8 42.2 %copy-start.3 = (bf16[1,1,6,256,256]{4,3,2,1,0:T(8,128)(2,1)S(1)}, bf16[1,1,6,256,256]{4,3,2,1,0:T(8,128)(2,1)}, u32[]{:S(2)}) copy-start(bf16[1,1,6,256,256]{4,3,2,1,0:T(8,128)(2,1)} %param.17) | copy-start | bytes 2359300
  3.8 42.2 %copy-start.4 = (f32[2,128,128]{2,1,0:T(8,128)S(1)}, f32[2,128,128]{2,1,0:T(8,128)}, u32[]{:S(2)}) copy-start(f32[2,128,128]{2,1,0:T(8,128)} %constant.36.clone.sub_tw) | copy-start | bytes 393220
  3.8 42.2 %copy-start.5 = (bf16[256,256]{1,0:T(8,128)(2,1)S(1)}, bf16[256,256]{1,0:T(8,128)(2,1)}, u32[]{:S(2)}) copy-start(bf16[256,256]{1,0:T(8,128)(2,1)} %constant.34.clone.pick_t) | copy-start | bytes 393220
  46.1 0.9 copy-start.6
  47.0 0.9 copy-start.7
  47.9 0.9 copy-start.8
  48.8 0.9 copy-start.9
  49.7 0.9 copy-start.10
  50.6 7.7 %copy-start.1 = (f32[2,512,512]{2,1,0:T(8,128)S(1)}, f32[2,512,512]{2,1,0:T(8,128)}, u32[]{:S(2)}) copy-start(f32[2,512,512]{2,1,0:T(8,128)} %field.3) | copy-start | bytes 6291460

commit v4 on v3

--- a/solution.py
+++ b/solution.py
@@ -38,67 +38,143 @@
     return pl.ds(0, MARGIN), pl.ds(MARGIN + TILE, MARGIN)
 
 
-def halo_kernel(field, meta, framed, metas, local_sems, send_sems, recv_sems, meta_send, meta_recv):
+def relays(down):
+    y = lax.rem(lax.axis_index("row"), 4)
+    return (y == 3, y == 2) if down == 1 else (y == 0, y == 1)
+
+
+def start_either(direct, detour, taken):
+    pl.when(taken)(detour.start)
+    pl.when(jnp.logical_not(taken))(direct.start)
+
+
+BESIDE = ((0, 1), (0, -1))
+PARTNERS = BESIDE + ((1, 0), (-1, 0), (2, 0), (-2, 0))
+ENDS = (0, TILE - MARGIN)
+MIDDLE = pl.ds(MARGIN, TILE - 2 * MARGIN)
+PIECE = MARGIN // 2
+
+
+def halo_kernel(
+    field, meta, framed, metas, relay, local_sems, side_send, side_recv, end_send, end_recv,
+    mid_send, mid_recv, relay_recv, on_send, corner_send, corner_recv, meta_send, meta_recv,
+):
+    greeted = PARTNERS + ((1, 1), (1, -1), (-1, 1), (-1, -1))
     barrier = pltpu.get_barrier_semaphore()
-    for dr, dc in NEIGHBOURS:
+    for dr, dc in greeted:
         pl.semaphore_signal(barrier, inc=1, device_id=shifted(dr, dc), device_id_type=MESH)
     own = pltpu.make_async_copy(
         field, framed.at[:, pl.ds(MARGIN, TILE), pl.ds(MARGIN, TILE)], local_sems.at[0]
     )
     own_meta = pltpu.make_async_copy(meta, metas.at[4], local_sems.at[1])
-    pl.semaphore_wait(barrier, len(NEIGHBOURS))
+    pl.semaphore_wait(barrier, len(greeted))
+
+    def remote(src, dst, send_sem, recv_sem, device):
+        return pltpu.make_async_remote_copy(
+            src_ref=src, dst_ref=dst, send_sem=send_sem, recv_sem=recv_sem,
+            device_id=device, device_id_type=MESH,
+        )
+
     copies = []
     for n, (dr, dc) in enumerate(NEIGHBOURS):
+        copies.append(
+            remote(
+                meta, metas.at[SIDES.index((-dr, -dc))], meta_send.at[n], meta_recv.at[n],
+                shifted(dr, dc),
+            )
+        )
+    ends, middles = {}, {}
+    for d, dr in enumerate((1, -1)):
         src_r, dst_r = edge_span(dr)
+        for e, lane in enumerate(ENDS):
+            ends[dr, e] = remote(
+                field.at[:, src_r, pl.ds(lane, MARGIN)],
+                framed.at[:, dst_r, pl.ds(MARGIN + lane, MARGIN)],
+                end_send.at[d, e], end_recv.at[d, e], shifted(dr, 0),
+            )
+            ends[dr, e].start()
+    for d, dr in enumerate((1, -1)):
+        src_r, dst_r = edge_span(dr)
+        taken, _ = relays(dr)
+        for i in range(2):
+            src = field.at[:, pl.ds(src_r.start + i * PIECE, PIECE), MIDDLE]
+            middles[dr, i] = remote(
+                src,
+                framed.at[:, pl.ds(dst_r.start + i * PIECE, PIECE), pl.ds(2 * MARGIN, MIDDLE.size)],
+                mid_send.at[d, i], mid_recv.at[d, i], shifted(dr, 0),
+            )
+            detour = remote(
+                src, relay.at[i], mid_send.at[d, i], relay_recv.at[i], shifted(-dr, 0)
+            )
+            start_either(middles[dr, i], detour, taken)
+    for d, (dr, dc) in enumerate(BESIDE):
         src_c, dst_c = edge_span(dc)
-        copies.append(
-            pltpu.make_async_remote_copy(
-                src_ref=field.at[:, src_r, src_c],
-                dst_ref=framed.at[:, dst_r, dst_c],
-                send_sem=send_sems.at[n],
-                recv_sem=recv_sems.at[n],
-                device_id=shifted(dr, dc),
-                device_id_type=MESH,
-            )
+        side = remote(
+            field.at[:, :, src_c], framed.at[:, pl.ds(MARGIN, TILE), dst_c],
+            side_send.at[d], side_recv.at[d], shifted(dr, dc),
         )
-        copies.append(
-            pltpu.make_async_remote_copy(
-                src_ref=meta,
-                dst_ref=metas.at[SIDES.index((-dr, -dc))],
-                send_sem=meta_send.at[n],
-                recv_sem=meta_recv.at[n],
-                device_id=shifted(dr, dc),
-                device_id_type=MESH,
-            )
-        )
+        copies.append(side)
     for copy in copies:
         copy.start()
     own.start()
     own_meta.start()
+    for d, dr in enumerate((1, -1)):
+        _, rows = edge_span(dr)
+        for e, dc in enumerate((-1, 1)):
+            ends[dr, e].wait()
+            _, lanes = edge_span(dc)
+            corner = remote(
+                framed.at[:, rows, pl.ds(MARGIN + ENDS[e], MARGIN)], framed.at[:, rows, lanes],
+                corner_send.at[d, e], corner_recv.at[d, e], shifted(0, dc),
+            )
+            corner.start()
+            copies.append(corner)
+    onward = {}
+    for d, dr in enumerate((1, -1)):
+        _, handed = relays(dr)
+        _, dst_r = edge_span(dr)
+        for i in range(2):
+            onward[dr, i] = remote(
+                relay.at[i],
+                framed.at[:, pl.ds(dst_r.start + i * PIECE, PIECE), pl.ds(2 * MARGIN, MIDDLE.size)],
+                on_send.at[i], mid_recv.at[d, i], shifted(2 * dr, 0),
+            )
+            arrived = remote(
+                relay.at[i], relay.at[i], on_send.at[i], relay_recv.at[i], shifted(2 * dr, 0)
+            )
+
+            @pl.when(handed)
+            def _():
+                arrived.wait_recv()
+                onward[dr, i].start()
+
     own.wait()
     own_meta.wait()
     for copy in copies:
         copy.wait()
+    for copy in middles.values():
+        copy.wait()
+    for (dr, _), copy in onward.items():
+        pl.when(relays(dr)[1])(copy.wait_send)
 
 
 def gather_frame(field, meta):
     any_spec = pl.BlockSpec(memory_space=pl.ANY)
     count = len(NEIGHBOURS)
     vmem = pl.BlockSpec(memory_space=pltpu.VMEM)
+    dma = pltpu.SemaphoreType.DMA
     return pl.pallas_call(
         halo_kernel,
         out_shape=(
             jax.ShapeDtypeStruct((2, EXT, EXT), jnp.float32),
             jax.ShapeDtypeStruct((9, 8, 128), jnp.int32),
         ),
-        in_specs=[any_spec, any_spec],
+        in_specs=[pl.BlockSpec(memory_space=pltpu.HBM), any_spec],
         out_specs=(vmem, any_spec),
         scratch_shapes=[
-            pltpu.SemaphoreType.DMA((2,)),
-            pltpu.SemaphoreType.DMA((count,)),
-            pltpu.SemaphoreType.DMA((count,)),
-            pltpu.SemaphoreType.DMA((count,)),
-            pltpu.SemaphoreType.DMA((count,)),
+            pltpu.VMEM((2, 2, PIECE, MIDDLE.size), jnp.float32),
+            dma((2,)), dma((2,)), dma((2,)), dma((2, 2)), dma((2, 2)), dma((2, 2)), dma((2, 2)),
+            dma((2,)), dma((2,)), dma((2, 2)), dma((2, 2)), dma((count,)), dma((count,)),
         ],
         compiler_params=pltpu.CompilerParams(
             collective_id=0, has_side_effects=True, vmem_limit_bytes=16 * 1024 * 1024
@@ -127,8 +203,9 @@
     for table in (right, right.T):
         high = table.astype(jnp.bfloat16)
         out += [high, (table - high.astype(np.float32)).astype(jnp.bfloat16)]
-    out += [pick.astype(jnp.bfloat16), pick.T.astype(jnp.bfloat16), lanes.copy(), subs.copy()]
-    return [jnp.asarray(t) for t in out]
+    out += [pick.astype(jnp.bfloat16), pick.T.astype(jnp.bfloat16)]
+    twists = np.concatenate([subs, lanes], 1)
+    return [jnp.asarray(np.stack(out)), jnp.asarray(twists)]
 
 
 def cat(parts, axis):
@@ -136,7 +213,7 @@
 
 
 def tile_kernel(
-    place, metas, framed, probe, amps, rh, rl, lh, ll, pick, pick_t, lane_tw, sub_tw,
+    place, metas, framed, probe, amps, mats, twists,
     grad, shade, sums,
     patch, xh, xl, yh, yl, amp, light, power, whole,
 ):
@@ -144,6 +221,8 @@
     dot = functools.partial(jnp.dot, preferred_element_type=f32)
     lane = lax.broadcasted_iota(jnp.int32, (1, HALF), 1)
     top, left = place[0], place[1]
+    rh, rl, lh, ll, pick, pick_t = (mats.at[n] for n in range(6))
+    sub_tw, lane_tw = twists.at[:, pl.ds(0, HALF), :], twists.at[:, pl.ds(HALF, 8), :]
 
     grad[...] = jnp.zeros_like(grad)
     sums[...] = jnp.zeros_like(sums)
@@ -166,7 +245,7 @@
 
     def light_slot(which, position):
         r = metas[which, 0, position] - top + 256
-        c = metas[which, 0, SLOTS + position] - left + 256
+        c = metas[which, 1, position] - left + 256
 
         @pl.when((r > 0) & (r < 768) & (c > 0) & (c < 768))
         def _():
@@ -185,7 +264,7 @@
             light_slot(which, position)
             return 0
 
-        lax.fori_loop(0, metas[which, 0, 2 * SLOTS], one, 0)
+        lax.fori_loop(0, metas[which, 2, 0], one, 0)
         return 0
 
     lax.fori_loop(0, 9, light_tile, 0)
@@ -196,7 +275,7 @@
 
     def visit(position, _):
         r = metas[4, 0, position] - top + MARGIN
-        c = metas[4, 0, SLOTS + position] - left + MARGIN
+        c = metas[4, 1, position] - left + MARGIN
         shift = lax.rem(c, HALF)
         base = pl.multiple_of(c - shift, HALF)
         down = lax.rem(r, 8)
@@ -344,7 +423,7 @@
                     grad[at] += block
         return 0
 
-    lax.fori_loop(0, metas[4, 0, 2 * SLOTS], visit, 0)
+    lax.fori_loop(0, metas[4, 2, 0], visit, 0)
 
 
 def tile_terms(place, metas, framed, probe, amps):
@@ -378,6 +457,11 @@
 
 
 RIM_SOURCE = {-1: (0, MARGIN), 0: (MARGIN, TILE), 1: (MARGIN + TILE, MARGIN)}
+CORNERS = (2, 3, 4, 5)
+PIECES = tuple(
+    piece for i in range(4) for piece in ((0, i), (1, i), (CORNERS[i], 0), (6, i), (7, i))
+)
+SLOT = (5, 4, 3, 2, 2, 2, 2)
 RIM_TARGET = {1: (0, MARGIN), 0: (0, TILE), -1: (TILE - MARGIN, MARGIN)}
 
 
@@ -440,9 +524,17 @@
     other = pl.multiple_of((1 - core) * HALF, HALF)
     to_pair = send(sums.at[:, pl.ds(other, HALF), :], pair_in, pair, red, 0)
     rims = []
-    for n, (dr, dc) in enumerate(NEIGHBOURS):
-        src = grad.at[:, pl.ds(*RIM_SOURCE[dr]), pl.ds(*RIM_SOURCE[dc])]
-        rims.append(send(src, ref_of(n), shifted(dr, dc), (rim_send, rim_recv), n))
+
+    def send_rims(count):
+        for n, i in PIECES[len(rims) : len(rims) + count]:
+            dr, dc = NEIGHBOURS[n]
+            (r0, rn), (c0, cn) = RIM_SOURCE[dr], RIM_SOURCE[dc]
+            size = rn if n in CORNERS else rn // 4
+            src = grad.at[:, pl.ds(r0 + i * size, size), pl.ds(c0, cn)]
+            dst = ref_of(n).at[:, pl.ds(i * size, size), :]
+            rims.append(send(src, dst, shifted(dr, dc), (rim_send, rim_recv), len(rims)))
+
+    send_rims(SLOT[0])
     for copy in locals_:
         copy.start()
 
@@ -450,34 +542,48 @@
     for i in range(0, HALF, ROWS):
         rows = pl.ds(i, ROWS)
         acc[:, rows, :] = sums[:, pl.ds(pl.multiple_of(half + i, ROWS), ROWS), :] + pair_in[:, rows, :]
+    turns = ((x, x_peers, y, y_peers), (y, y_peers, x, x_peers))
     copies = []
     for d in range(1, 4):
-        at = pl.multiple_of(lax.rem(x + d, 4) * 32, 32)
-        copies.append(send(acc.at[:, pl.ds(at, 32), :], x_in.at[d - 1], x_peers[d - 1], red, d))
+        for h, (one, one_peers, _, _) in enumerate(turns):
+            at = pl.multiple_of(lax.rem(one + d, 4) * 32, 32)
+            src = acc.at[:, pl.ds(at, 32), pl.ds(h * HALF, HALF)]
+            copies.append(send(src, x_in.at[h, d - 1], one_peers[d - 1], red, 3 * h + d))
+    send_rims(SLOT[1])
     for copy in copies:
         copy.wait()
-    x_at = pl.multiple_of(x * 32, 32)
-    mine = acc[:, pl.ds(x_at, 32), :]
-    for d in range(3):
-        mine = mine + x_in[d]
-    acc[:, pl.ds(x_at, 32), :] = mine
     copies = []
-    for d in range(1, 4):
-        at = pl.multiple_of(x_at + lax.rem(y + d, 4) * 8, 8)
-        copies.append(send(acc.at[:, pl.ds(at, 8), :], y_in.at[d - 1], y_peers[d - 1], red, 3 + d))
+    ats = []
+    for h, (one, _, two, two_peers) in enumerate(turns):
+        lanes = pl.ds(h * HALF, HALF)
+        at = pl.multiple_of(one * 32, 32)
+        mine = acc[:, pl.ds(at, 32), lanes]
+        for d in range(3):
+            mine = mine + x_in[h, d]
+        acc[:, pl.ds(at, 32), lanes] = mine
+        ats.append((at, pl.multiple_of(at + two * 8, 8)))
+        for d in range(1, 4):
+            to = pl.multiple_of(at + lax.rem(two + d, 4) * 8, 8)
+            src = acc.at[:, pl.ds(to, 8), lanes]
+            copies.append(send(src, y_in.at[h, d - 1], two_peers[d - 1], red, 6 + 3 * h + d))
+    send_rims(SLOT[2])
     for copy in copies:
         copy.wait()
-    y_at = pl.multiple_of(x_at + y * 8, 8)
-    mine = acc[:, pl.ds(y_at, 8), :]
-    for d in range(3):
-        mine = mine + y_in[d]
+    halves = []
+    for h in range(2):
+        part = acc[:, pl.ds(ats[h][1], 8), pl.ds(h * HALF, HALF)]
+        for d in range(3):
+            part = part + y_in[h, d]
+        halves.append(part)
+    mine = jnp.concatenate(halves, 2)
     rows_out[...] = jnp.zeros_like(rows_out)
     for r in range(8):
         for p in range(5):
             rows_out[r, pl.ds(p, 1), :] = mine[p, r : r + 1, :]
     copies = []
     for d in range(1, 8):
-        copies.append(send(rows_out.at[lax.rem(z + d, 8)], z_in.at[d - 1], z_peers[d - 1], red, 6 + d))
+        copies.append(send(rows_out.at[lax.rem(z + d, 8)], z_in.at[d - 1], z_peers[d - 1], red, 12 + d))
+    send_rims(SLOT[3])
     for copy in copies:
         copy.wait()
     total = rows_out[z]
@@ -489,21 +595,29 @@
     for d in range(1, 8):
         copies.append(send(row_new, rows_in.at[z], z_peers[d - 1], put, d))
     rows_in[z] = row_new[...]
+    send_rims(SLOT[4])
     for copy in copies:
         copy.wait()
-    at = pl.multiple_of(half + y_at, 8)
-    for p in range(4):
-        spread[p, pl.ds(at, 8), :] = jnp.concatenate([rows_in[r, pl.ds(p, 1), :] for r in range(8)], 0)
     copies = []
-    block = spread.at[:, pl.ds(at, 8), :]
-    for d in range(1, 4):
-        copies.append(send(block, block, y_peers[d - 1], put, 7 + d))
+    for h in range(2):
+        at, lanes = pl.multiple_of(half + ats[h][1], 8), pl.ds(h * HALF, HALF)
+        for p in range(4):
+            spread[p, pl.ds(at, 8), lanes] = jnp.concatenate(
+                [rows_in[r, pl.ds(p, 1), lanes] for r in range(8)], 0
+            )
+        block = spread.at[:, pl.ds(at, 8), lanes]
+        for d in range(1, 4):
+            copies.append(send(block, block, turns[h][3][d - 1], put, 7 + 3 * h + d))
+    send_rims(SLOT[5])
     for copy in copies:
         copy.wait()
-    block = spread.at[:, pl.ds(pl.multiple_of(half + x_at, 32), 32), :]
     copies = []
     for d in range(1, 4):
-        copies.append(send(block, block, x_peers[d - 1], put, 10 + d))
+        for h in range(2):
+            at = pl.multiple_of(half + ats[h][0], 32)
+            block = spread.at[:, pl.ds(at, 32), pl.ds(h * HALF, HALF)]
+            copies.append(send(block, block, turns[h][1][d - 1], put, 13 + 3 * h + d))
+    send_rims(SLOT[6])
     for copy in copies:
         copy.wait()
     block = spread.at[:, pl.ds(half, HALF), :]
@@ -511,8 +625,9 @@
 
     for copy in locals_:
         copy.wait()
+    for copy in rims:
+        copy.wait()
     for n, (dr, dc) in enumerate(NEIGHBOURS):
-        rims[n].wait()
         (r0, rn), (c0, cn) = RIM_TARGET[dr], RIM_TARGET[dc]
         for i in range(0, rn, 64):
             rows = pl.ds(r0 + i, 64)
@@ -549,15 +664,15 @@
             pltpu.VMEM((2, 2, TILE, MARGIN), f32),
             pltpu.VMEM((4, 2, MARGIN, MARGIN), f32),
             pltpu.VMEM((5, HALF, EDGE), f32),
-            pltpu.VMEM((3, 5, 32, EDGE), f32),
-            pltpu.VMEM((3, 5, 8, EDGE), f32),
+            pltpu.VMEM((2, 3, 5, 32, HALF), f32),
+            pltpu.VMEM((2, 3, 5, 8, HALF), f32),
             pltpu.VMEM((7, 8, EDGE), f32),
             pltpu.VMEM((5, HALF, EDGE), f32),
             pltpu.VMEM((8, 8, EDGE), f32),
             pltpu.VMEM((8, EDGE), f32),
             pltpu.VMEM((8, 8, EDGE), f32),
             pltpu.VMEM((4, EDGE, EDGE), f32),
-            dma((1,)), dma((8,)), dma((8,)), dma((14,)), dma((14,)), dma((14,)), dma((14,)),
+            dma((1,)), dma((len(PIECES),)), dma((len(PIECES),)), dma((20,)), dma((20,)), dma((20,)), dma((20,)),
         ],
         compiler_params=pltpu.CompilerParams(
             collective_id=1, has_side_effects=True, vmem_limit_bytes=32 * 1024 * 1024
@@ -568,8 +683,7 @@
 
 def on_device(field, probe, offsets, counts, amps):
     row, col = lax.axis_index("row"), lax.axis_index("col")
-    meta = jnp.concatenate([offsets.reshape(2 * SLOTS), counts.reshape(1)])
-    meta = jnp.broadcast_to(jnp.pad(meta, (0, 128 - 2 * SLOTS - 1))[None], (8, 128))
+    meta = jnp.pad(offsets[0, 0], ((0, 6), (0, 128 - SLOTS))) + jnp.pad(counts, ((2, 5), (0, 127)))
     framed, metas = gather_frame(field, meta)
     place = jnp.stack([row * TILE, col * TILE]).astype(jnp.int32)
     grad, shade, sums = tile_terms(place, metas, framed, probe, amps[0, 0])

time: 134 us -> 117 us (0.87)
  Pallas kernels: 123 us -> 110 us
  local copies, waits for them, and re-layouts: 9.19 us -> 5.03 us
    pallas_call x1, Pallas kernels: 42.2 us -> 32.5 us  [gather_frame(): pl.pallas_call(halo_kernel, out_shape=(jax.ShapeDtypeStruct((2, EXT, EXT)...]
    unnamed x26 -> x14, local copies, waits for them, and re-layouts: 8.42 us -> 5.03 us
    pallas_call x1, Pallas kernels: 72.7 us -> 70.3 us  [fold(): pl.pallas_call(fold_kernel, out_shape=(jax.ShapeDtypeStruct((2, TILE, TIL...]
where the time goes in v4:
time: 117 us
  Pallas kernels  110 us (94%)
  local copies, waits for them, and re-layouts  5.03 us (4%)
  between operations  1.35 us (1%)
    pallas_call x1, Pallas kernels, fold(): pl.pallas_call(fold_kernel, out_shape=(jax.ShapeDtypeStruct((2, TILE, TIL...  70.3 us
    pallas_call x1, Pallas kernels, gather_frame(): pl.pallas_call(halo_kernel, out_shape=(jax.ShapeDtypeStruct((2, EXT, EXT)...  32.5 us
    pallas_call x1, Pallas kernels, tile_terms(): pl.pallas_call(tile_kernel, out_shape=(jax.ShapeDtypeStruct((2, EXT, EXT)...  6.9 us
    unnamed x14, local copies, waits for them, and re-layouts  5.03 us

profile of v4, /device:TPU:1, one launch (start us, length us, event | category | flops | bytes accessed | tf_op | source)
XLA Modules:
  0.0 116.8 jit_solution(1546462528051597921)
XLA Ops:
  1.3 0.1 pad_add_fusion.1.place
  1.4 0.7 pad_add_fusion.meta
  2.0 0.0 copy-start
  2.0 1.6 %copy-done = f32[2,512,512]{2,1,0:T(8,128)S(1)} copy-done((f32[2,512,512]{2,1,0:T(8,128)S(1)}, f32[2,512,512]{2,1,0:T(8,128)}, u32[]{:S(2)}) %copy-start) | copy-done | bytes 2097176
  3.6 0.0 copy-start.2
  3.6 0.0 copy-start.3
  3.6 0.0 copy-start.5
  3.6 32.5 %halo.1 = (f32[2,768,768]{2,1,0:T(8,128)S(1)}, s32[9,8,128]{2,1,0:T(8,128)S(1)}) custom-call(f32[2,512,512]{2,1,0:T(8,128)S(1)} %copy-done, s32[8,128]{1,0:T(8,128)S(1)} %pad_add_fusion.meta), custom_call_target="tpu_custom_call" | custom-call | tf_op jit(solution)/shard_map/halo/pallas_call | solution.py:166
  36.2 0.0 copy-done.2
  36.2 0.0 copy-done.3
  36.2 0.0 copy-done.5
  36.2 0.0 copy-start.4
  36.2 1.1 copy-done.4
  37.4 0.0 copy-start.1
  37.4 6.9 %tile.1 = (f32[2,768,768]{2,1,0:T(8,128)S(1)}, f32[512,512]{1,0:T(8,128)S(1)}, f32[5,256,256]{2,1,0:T(8,128)S(1)}) custom-call(s32[2]{0:T(128)S(1)} %pad_add_fusion.1.place, s32[9,8,128]{2,1,0:T(8,128)S(1)} %get-tuple-element.7.metas, f32[2,768,768]{2,1,0:T(8,128)S(1)} %get-tuple-element.8.framed, f32[2,2,256,256]{3,2,1,0:T(8,128)S(1)} %copy-done.2, ...), custom_call_target="tpu_custom_call" | custom-call | tf_op jit(solution)/shard_map/tile/pallas_call | solution.py:434
  44.3 0.0 copy-done.1
  44.3 70.3 %fold.1 = (f32[2,512,512]{2,1,0:T(8,128)S(1)}, f32[2,2,256,256]{3,2,1,0:T(8,128)S(1)}) custom-call(f32[2,768,768]{2,1,0:T(8,128)S(1)} %get-tuple-element.9.grad, f32[2,512,512]{2,1,0:T(8,128)S(1)} %copy-done.1, f32[512,512]{1,0:T(8,128)S(1)} %get-tuple-element.10.shade, f32[5,256,256]{2,1,0:T(8,128)S(1)} %get-tuple-element.11.sums, ...), custom_call_target="tpu_custom_call" | custom-call | tf_op jit(solution)/shard_map/fold/pallas_call | solution.py:653
  114.6 1.3 %copy.12 = f32[2,512,512]{2,1,0:T(8,128)} copy(f32[2,512,512]{2,1,0:T(8,128)S(1)} %get-tuple-element.14) | data formatting | bytes 4194304
  115.9 1.0 copy.13
Async XLA Ops:
  2.0 1.6 %copy-start = (f32[2,512,512]{2,1,0:T(8,128)S(1)}, f32[2,512,512]{2,1,0:T(8,128)}, u32[]{:S(2)}) copy-start(f32[2,512,512]{2,1,0:T(8,128)} %field.3) | copy-start | bytes 6291460
  3.6 32.6 %copy-start.2 = (f32[2,2,256,256]{3,2,1,0:T(8,128)S(1)}, f32[2,2,256,256]{3,2,1,0:T(8,128)}, u32[]{:S(2)}) copy-start(f32[2,2,256,256]{3,2,1,0:T(8,128)} %probe.3) | copy-start | bytes 3145732
  3.6 32.6 %copy-start.3 = (bf16[1,1,6,256,256]{4,3,2,1,0:T(8,128)(2,1)S(1)}, bf16[1,1,6,256,256]{4,3,2,1,0:T(8,128)(2,1)}, u32[]{:S(2)}) copy-start(bf16[1,1,6,256,256]{4,3,2,1,0:T(8,128)(2,1)} %param.11) | copy-start | bytes 2359300
  3.6 32.6 %copy-start.5 = (f32[2,136,128]{2,1,0:T(8,128)S(1)}, f32[2,136,128]{2,1,0:T(8,128)}, u32[]{:S(2)}) copy-start(f32[2,136,128]{2,1,0:T(8,128)} %constant.18.clone.twists) | copy-start | bytes 417796
  36.2 1.1 copy-start.4
  37.4 6.9 %copy-start.1 = (f32[2,512,512]{2,1,0:T(8,128)S(1)}, f32[2,512,512]{2,1,0:T(8,128)}, u32[]{:S(2)}) copy-start(f32[2,512,512]{2,1,0:T(8,128)} %field.3) | copy-start | bytes 6291460

commit v5 on v4

--- a/solution.py
+++ b/solution.py
@@ -215,7 +215,7 @@
 def tile_kernel(
     place, metas, framed, probe, amps, mats, twists,
     grad, shade, sums,
-    patch, xh, xl, yh, yl, amp, light, power, whole,
+    patch, xh, xl, yh, yl, amp, light, power, whole, back, far, near, update,
 ):
     f32, bf16 = jnp.float32, jnp.bfloat16
     dot = functools.partial(jnp.dot, preferred_element_type=f32)
@@ -271,8 +271,6 @@
     for i in range(0, TILE, ROWS):
         shade[pl.ds(i, ROWS), :] = 1.0 / (light[pl.ds(256 + i, ROWS), pl.ds(256, TILE)] + 1.0)
 
-    right_hhl = cat([rh[...], rh[...], rl[...]], 0)
-
     def visit(position, _):
         r = metas[4, 0, position] - top + MARGIN
         c = metas[4, 1, position] - left + MARGIN
@@ -283,58 +281,69 @@
         up = lax.rem(ROWS + 8 - down, ROWS + 8)
         back_shift = lax.rem(HALF - shift, HALF)
         keep = lane < HALF - shift
-        picked = dot(pick[...], amps[position]).astype(bf16)
-        amp[...] = dot(picked, pick_t[...])
-
-        for i in range(0, EDGE, ROWS):
-            s = pl.ds(i, ROWS)
-            planes = []
-            for plane in range(2):
-                rolled = [
-                    pltpu.roll(
+        cosine_l, sine_l = lane_tw[0, :1, :], lane_tw[1, :1, :]
+
+        def block_of(k, part, row=0, rows=EDGE):
+            return pl.ds((2 * k + part) * EDGE + row, rows)
+
+        def put(high_ref, low_ref, at, value):
+            high, low = split(value)
+            high_ref[at] = high
+            low_ref[at] = low
+
+        def take_patch():
+            for i in range(0, EDGE, ROWS):
+                s = pl.ds(i, ROWS)
+                for plane in range(2):
+                    rolled = [
                         pltpu.roll(
-                            framed[
-                                plane, pl.ds(first + i, ROWS + 8), pl.ds(base + b * HALF, HALF)
-                            ],
-                            up,
-                            0,
-                        )[:ROWS],
-                        back_shift,
-                        1,
-                    )
-                    for b in range(3)
-                ]
-                planes.append(
-                    (jnp.where(keep, rolled[0], rolled[1]), jnp.where(keep, rolled[1], rolled[2]))
-                )
-            for plane in range(2):
-                for h in range(2):
-                    patch[plane, s, pl.ds(h * HALF, HALF)] = planes[plane][h]
-            for k in range(2):
+                            pltpu.roll(
+                                framed[
+                                    plane, pl.ds(first + i, ROWS + 8), pl.ds(base + b * HALF, HALF)
+                                ],
+                                up,
+                                0,
+                            )[:ROWS],
+                            back_shift,
+                            1,
+                        )
+                        for b in range(3)
+                    ]
+                    patch[plane, s, :HALF] = jnp.where(keep, rolled[0], rolled[1])
+                    patch[plane, s, HALF:] = jnp.where(keep, rolled[1], rolled[2])
+
+        def wave(k):
+            for i in range(0, EDGE, ROWS):
+                s = pl.ds(i, ROWS)
                 wr, wi = [], []
                 for h in range(2):
-                    pr, pi = (probe[p, k, s, pl.ds(h * HALF, HALF)] for p in range(2))
-                    wr.append(pr * planes[0][h] - pi * planes[1][h])
-                    wi.append(pr * planes[1][h] + pi * planes[0][h])
-                cosine, sine = lane_tw[0, :1, :], lane_tw[1, :1, :]
+                    cols = pl.ds(h * HALF, HALF)
+                    pr, pi = probe[0, k, s, cols], probe[1, k, s, cols]
+                    vr, vi = patch[0, s, cols], patch[1, s, cols]
+                    wr.append(pr * vr - pi * vi)
+                    wi.append(pr * vi + pi * vr)
                 dr, di = wr[0] - wr[1], wi[0] - wi[1]
-                for part, value in (
-                    (0, cat([wr[0] + wr[1], wi[0] + wi[1]], 1)),
-                    (1, cat([dr * cosine + di * sine, di * cosine - dr * sine], 1)),
-                ):
-                    high, low = split(value)
-                    at = pl.ds((2 * k + part) * EDGE + i, ROWS)
-                    xh[at, :] = high
-                    xl[at, :] = low
-
-        whole[...] = dot(cat([xh[...], xl[...], xh[...]], 1), right_hhl)
-        for k in range(2):
+                put(xh, xl, (block_of(k, 0, i, ROWS), slice(None)), cat([wr[0] + wr[1], wi[0] + wi[1]], 1))
+                put(
+                    xh, xl, (block_of(k, 1, i, ROWS), slice(None)),
+                    cat([dr * cosine_l + di * sine_l, di * cosine_l - dr * sine_l], 1),
+                )
+
+        def columns(k, high, low, to):
+            s = pl.ds(2 * k * EDGE, 2 * EDGE)
+            table = cat([high[...], high[...], low[...]], 0)
+            to[s, :] = dot(cat([xh[s, :], xl[s, :], xh[s, :]], 1), table)
+
+        def rows(k, part, high, low, to):
+            n = 2 * k + part
+            table = cat([high[...], high[...], low[...]], 1)
+            to[n] = dot(table, cat([yh[n], yl[n], yh[n]], 0))
+
+        def halve_rows(k):
             for i in range(0, HALF, ROWS):
                 res = []
                 for row in (i, HALF + i):
-                    parts = [
-                        whole[pl.ds((2 * k + part) * EDGE + row, ROWS), :] for part in range(2)
-                    ]
+                    parts = [whole[block_of(k, part, row, ROWS), :] for part in range(2)]
                     res.append(
                         (
                             cat([parts[0][:, :HALF], parts[1][:, :HALF]], 1),
@@ -350,77 +359,93 @@
                     (1, dr * cosine + di * sine, di * cosine - dr * sine),
                 ):
                     for start, value in ((0, real), (HALF, imag)):
-                        high, low = split(value)
-                        at = (2 * k + part, pl.ds(start + i, ROWS), slice(None))
-                        yh[at] = high
-                        yl[at] = low
-
-        for part in range(2):
-            far = [
-                dot(
-                    cat([lh[...], lh[...], ll[...]], 1),
-                    cat([yh[2 * k + part], yl[2 * k + part], yh[2 * k + part]], 0),
-                )
-                for k in range(2)
-            ]
+                        put(yh, yl, (2 * k + part, pl.ds(start + i, ROWS), slice(None)), value)
+
+        def scale(part):
             for i in range(0, HALF, ROWS):
-                pieces = [(f[i : i + ROWS], f[HALF + i : HALF + i + ROWS]) for f in far]
+                pieces = [
+                    (far[2 * k + part, pl.ds(i, ROWS), :], far[2 * k + part, pl.ds(HALF + i, ROWS), :])
+                    for k in range(2)
+                ]
                 total = sum(a * a + b * b for a, b in pieces)
                 total = jnp.maximum(total * (1.0 / 65536.0), 0.25)
                 factor = amp[pl.ds(part * HALF + i, ROWS), :] * lax.rsqrt(total) - 1.0
                 factor = factor * (1.0 / 65536.0)
                 for k in range(2):
                     for start, value in ((0, pieces[k][0]), (HALF, pieces[k][1])):
-                        high, low = split(value * factor)
                         at = (2 * k + part, pl.ds(start + i, ROWS), slice(None))
-                        yh[at] = high
-                        yl[at] = low
-        for k in range(2):
-            near = [
-                dot(
-                    cat([rh[...], rh[...], rl[...]], 1),
-                    cat([yh[2 * k + part], yl[2 * k + part], yh[2 * k + part]], 0),
+                        put(yh, yl, at, value * factor)
+
+        def join_rows(k):
+            for i in range(0, HALF, ROWS):
+                (ar, ai), (br, bi) = (
+                    (near[2 * k + part, pl.ds(i, ROWS), :], near[2 * k + part, pl.ds(HALF + i, ROWS), :])
+                    for part in range(2)
                 )
-                for part in range(2)
-            ]
-            for i in range(0, HALF, ROWS):
-                (ar, ai), (br, bi) = ((f[i : i + ROWS], f[HALF + i : HALF + i + ROWS]) for f in near)
                 cosine = cat([sub_tw[0, pl.ds(i, ROWS), :]] * 2, 1)
                 sine = cat([sub_tw[1, pl.ds(i, ROWS), :]] * 2, 1)
                 br, bi = br * cosine - bi * sine, bi * cosine + br * sine
                 for row, real, imag in ((i, ar + br, ai + bi), (HALF + i, ar - br, ai - bi)):
                     for part in range(2):
                         cols = slice(part * HALF, (part + 1) * HALF)
-                        high, low = split(cat([real[:, cols], imag[:, cols]], 1))
-                        at = pl.ds((2 * k + part) * EDGE + row, ROWS)
-                        xh[at, :] = high
-                        xl[at, :] = low
-
-        left_hhl = cat([lh[...], lh[...], ll[...]], 0)
-        whole[...] = dot(cat([xh[...], xl[...], xh[...]], 1), left_hhl)
-        for i in range(0, EDGE, ROWS):
-            s = pl.ds(i, ROWS)
-            update = [[0.0, 0.0], [0.0, 0.0]]
-            cosine, sine = lane_tw[0, :1, :], lane_tw[1, :1, :]
-            for k in range(2):
-                parts = [whole[pl.ds((2 * k + part) * EDGE + i, ROWS), :] for part in range(2)]
+                        put(
+                            xh, xl, (block_of(k, part, row, ROWS), slice(None)),
+                            cat([real[:, cols], imag[:, cols]], 1),
+                        )
+
+        def gather_sums(k):
+            for i in range(0, EDGE, ROWS):
+                s = pl.ds(i, ROWS)
+                parts = [back[block_of(k, part, i, ROWS), :] for part in range(2)]
                 ar, ai = parts[0][:, :HALF], parts[0][:, HALF:]
                 br, bi = parts[1][:, :HALF], parts[1][:, HALF:]
-                br, bi = br * cosine - bi * sine, bi * cosine + br * sine
+                br, bi = br * cosine_l - bi * sine_l, bi * cosine_l + br * sine_l
+                changed = [[None, None], [None, None]]
                 for h, real, imag in ((0, ar + br, ai + bi), (1, ar - br, ai - bi)):
                     cols = pl.ds(h * HALF, HALF)
                     pr, pi = probe[0, k, s, cols], probe[1, k, s, cols]
-                    update[0][h] += pr * real + pi * imag
-                    update[1][h] += pr * imag - pi * real
                     vr, vi = patch[0, s, cols], patch[1, s, cols]
+                    ur, ui = pr * real + pi * imag, pr * imag - pi * real
                     sums[k, s, cols] += vr * real + vi * imag
                     sums[2 + k, s, cols] += vr * imag - vi * real
                     if k == 0:
+                        update[0, s, cols] = ur
+                        update[1, s, cols] = ui
                         sums[4, s, cols] += vr * vr + vi * vi
-            for plane in range(2):
-                for b, block in enumerate(spread(*update[plane], down, shift)):
-                    at = (plane, pl.ds(first + i, ROWS + 8), pl.ds(base + b * HALF, HALF))
-                    grad[at] += block
+                    else:
+                        changed[0][h] = update[0, s, cols] + ur
+                        changed[1][h] = update[1, s, cols] + ui
+                if k == 1:
+                    for plane in range(2):
+                        for b, block in enumerate(spread(*changed[plane], down, shift)):
+                            at = (plane, pl.ds(first + i, ROWS + 8), pl.ds(base + b * HALF, HALF))
+                            grad[at] += block
+
+        take_patch()
+        wave(0)
+        columns(0, rh, rl, whole)
+        wave(1)
+        columns(1, rh, rl, whole)
+        picked = dot(pick[...], amps[position]).astype(bf16)
+        halve_rows(0)
+        rows(0, 0, lh, ll, far)
+        rows(0, 1, lh, ll, far)
+        amp[...] = dot(picked, pick_t[...])
+        halve_rows(1)
+        rows(1, 0, lh, ll, far)
+        rows(1, 1, lh, ll, far)
+        scale(0)
+        rows(0, 0, rh, rl, near)
+        rows(1, 0, rh, rl, near)
+        scale(1)
+        rows(0, 1, rh, rl, near)
+        rows(1, 1, rh, rl, near)
+        join_rows(0)
+        columns(0, lh, ll, back)
+        join_rows(1)
+        columns(1, lh, ll, back)
+        gather_sums(0)
+        gather_sums(1)
         return 0
 
     lax.fori_loop(0, metas[4, 2, 0], visit, 0)
@@ -450,6 +475,10 @@
             pltpu.VMEM((LIT, LIT_PAD), f32),
             pltpu.VMEM((EDGE, EDGE), f32),
             pltpu.VMEM((4 * EDGE, EDGE), f32),
+            pltpu.VMEM((4 * EDGE, EDGE), f32),
+            pltpu.VMEM((4, EDGE, EDGE), f32),
+            pltpu.VMEM((4, EDGE, EDGE), f32),
+            pltpu.VMEM((2, EDGE, EDGE), f32),
         ],
         compiler_params=pltpu.CompilerParams(vmem_limit_bytes=40 * 1024 * 1024),
         name="tile",
@@ -576,10 +605,7 @@
             part = part + y_in[h, d]
         halves.append(part)
     mine = jnp.concatenate(halves, 2)
-    rows_out[...] = jnp.zeros_like(rows_out)
-    for r in range(8):
-        for p in range(5):
-            rows_out[r, pl.ds(p, 1), :] = mine[p, r : r + 1, :]
+    rows_out[...] = jnp.swapaxes(jnp.concatenate([mine, jnp.zeros((3, 8, EDGE), f32)], 0), 0, 1)
     copies = []
     for d in range(1, 8):
         copies.append(send(rows_out.at[lax.rem(z + d, 8)], z_in.at[d - 1], z_peers[d - 1], red, 12 + d))
@@ -598,13 +624,11 @@
     send_rims(SLOT[4])
     for copy in copies:
         copy.wait()
+    planes = jnp.swapaxes(rows_in[...], 0, 1)[:4]
     copies = []
     for h in range(2):
         at, lanes = pl.multiple_of(half + ats[h][1], 8), pl.ds(h * HALF, HALF)
-        for p in range(4):
-            spread[p, pl.ds(at, 8), lanes] = jnp.concatenate(
-                [rows_in[r, pl.ds(p, 1), lanes] for r in range(8)], 0
-            )
+        spread[:, pl.ds(at, 8), lanes] = planes[:, :, h * HALF : (h + 1) * HALF]
         block = spread.at[:, pl.ds(at, 8), lanes]
         for d in range(1, 4):
             copies.append(send(block, block, turns[h][3][d - 1], put, 7 + 3 * h + d))
@@ -618,20 +642,8 @@
             block = spread.at[:, pl.ds(at, 32), pl.ds(h * HALF, HALF)]
             copies.append(send(block, block, turns[h][1][d - 1], put, 13 + 3 * h + d))
     send_rims(SLOT[6])
-    for copy in copies:
-        copy.wait()
-    block = spread.at[:, pl.ds(half, HALF), :]
-    last = send(block, block, pair, put, 0)
-
     for copy in locals_:
         copy.wait()
-    for copy in rims:
-        copy.wait()
-    for n, (dr, dc) in enumerate(NEIGHBOURS):
-        (r0, rn), (c0, cn) = RIM_TARGET[dr], RIM_TARGET[dc]
-        for i in range(0, rn, 64):
-            rows = pl.ds(r0 + i, 64)
-            base[:, rows, pl.ds(c0, cn)] += ref_of(n)[:, pl.ds(i, 64), :] * shade[rows, pl.ds(c0, cn)]
     for i in range(0, TILE, ROWS):
         rows = pl.ds(i, ROWS)
         for c in range(2):
@@ -639,6 +651,18 @@
                 base[c, rows, :]
                 + grad[c, pl.ds(MARGIN + i, ROWS), pl.ds(MARGIN, TILE)] * shade[rows, :]
             )
+    for copy in copies:
+        copy.wait()
+    block = spread.at[:, pl.ds(half, HALF), :]
+    last = send(block, block, pair, put, 0)
+
+    for copy in rims:
+        copy.wait()
+    for n, (dr, dc) in enumerate(NEIGHBOURS):
+        (r0, rn), (c0, cn) = RIM_TARGET[dr], RIM_TARGET[dc]
+        for i in range(0, rn, 64):
+            rows = pl.ds(r0 + i, 64)
+            object_out[:, rows, pl.ds(c0, cn)] += ref_of(n)[:, pl.ds(i, 64), :] * shade[rows, pl.ds(c0, cn)]
     last.wait()
     for c in range(2):
         for k in range(2):

time: 117 us -> 115 us (0.983)
  Pallas kernels: 110 us -> 108 us
    pallas_call x1, Pallas kernels: 70.3 us -> 69.1 us  [fold(): pl.pallas_call(fold_kernel, out_shape=(jax.ShapeDtypeStruct((2, TILE, TIL...]
where the time goes in v5:
time: 115 us
  Pallas kernels  108 us (94%)
  local copies, waits for them, and re-layouts  5.03 us (4%)
  between operations  1.35 us (1%)
    pallas_call x1, Pallas kernels, fold(): pl.pallas_call(fold_kernel, out_shape=(jax.ShapeDtypeStruct((2, TILE, TIL...  69.1 us
    pallas_call x1, Pallas kernels, gather_frame(): pl.pallas_call(halo_kernel, out_shape=(jax.ShapeDtypeStruct((2, EXT, EXT)...  32.5 us
    pallas_call x1, Pallas kernels, tile_terms(): pl.pallas_call(tile_kernel, out_shape=(jax.ShapeDtypeStruct((2, EXT, EXT)...  6.31 us
    unnamed x14, local copies, waits for them, and re-layouts  5.03 us

profile of v5, /device:TPU:1, one launch (start us, length us, event | category | flops | bytes accessed | tf_op | source)
XLA Modules:
  0.0 115.1 jit_solution(11631268725607943814)
XLA Ops:
  1.3 0.1 pad_add_fusion.1.place
  1.4 0.7 pad_add_fusion.meta
  2.0 0.0 copy-start
  2.0 1.6 %copy-done = f32[2,512,512]{2,1,0:T(8,128)S(1)} copy-done((f32[2,512,512]{2,1,0:T(8,128)S(1)}, f32[2,512,512]{2,1,0:T(8,128)}, u32[]{:S(2)}) %copy-start) | copy-done | bytes 2097176
  3.6 0.0 copy-start.2
  3.6 0.0 copy-start.3
  3.6 0.0 copy-start.5
  3.6 32.5 %halo.1 = (f32[2,768,768]{2,1,0:T(8,128)S(1)}, s32[9,8,128]{2,1,0:T(8,128)S(1)}) custom-call(f32[2,512,512]{2,1,0:T(8,128)S(1)} %copy-done, s32[8,128]{1,0:T(8,128)S(1)} %pad_add_fusion.meta), custom_call_target="tpu_custom_call" | custom-call | tf_op jit(solution)/shard_map/halo/pallas_call | solution.py:166
  36.2 0.0 copy-done.2
  36.2 0.0 copy-done.3
  36.2 0.0 copy-done.5
  36.2 0.0 copy-start.4
  36.2 1.1 copy-done.4
  37.4 0.0 copy-start.1
  37.4 6.3 %tile.1 = (f32[2,768,768]{2,1,0:T(8,128)S(1)}, f32[512,512]{1,0:T(8,128)S(1)}, f32[5,256,256]{2,1,0:T(8,128)S(1)}) custom-call(s32[2]{0:T(128)S(1)} %pad_add_fusion.1.place, s32[9,8,128]{2,1,0:T(8,128)S(1)} %get-tuple-element.7.metas, f32[2,768,768]{2,1,0:T(8,128)S(1)} %get-tuple-element.8.framed, f32[2,2,256,256]{3,2,1,0:T(8,128)S(1)} %copy-done.2, ...), custom_call_target="tpu_custom_call" | custom-call | tf_op jit(solution)/shard_map/tile/pallas_call | solution.py:459
  43.7 0.0 copy-done.1
  43.7 69.1 %fold.1 = (f32[2,512,512]{2,1,0:T(8,128)S(1)}, f32[2,2,256,256]{3,2,1,0:T(8,128)S(1)}) custom-call(f32[2,768,768]{2,1,0:T(8,128)S(1)} %get-tuple-element.9.grad, f32[2,512,512]{2,1,0:T(8,128)S(1)} %copy-done.1, f32[512,512]{1,0:T(8,128)S(1)} %get-tuple-element.10.shade, f32[5,256,256]{2,1,0:T(8,128)S(1)} %get-tuple-element.11.sums, ...), custom_call_target="tpu_custom_call" | custom-call | tf_op jit(solution)/shard_map/fold/pallas_call | solution.py:677
  112.8 1.3 %copy.12 = f32[2,512,512]{2,1,0:T(8,128)} copy(f32[2,512,512]{2,1,0:T(8,128)S(1)} %get-tuple-element.14) | data formatting | bytes 4194304
  114.1 1.0 copy.13
Async XLA Ops:
  2.0 1.6 %copy-start = (f32[2,512,512]{2,1,0:T(8,128)S(1)}, f32[2,512,512]{2,1,0:T(8,128)}, u32[]{:S(2)}) copy-start(f32[2,512,512]{2,1,0:T(8,128)} %field.3) | copy-start | bytes 6291460
  3.6 32.6 %copy-start.2 = (f32[2,2,256,256]{3,2,1,0:T(8,128)S(1)}, f32[2,2,256,256]{3,2,1,0:T(8,128)}, u32[]{:S(2)}) copy-start(f32[2,2,256,256]{3,2,1,0:T(8,128)} %probe.3) | copy-start | bytes 3145732
  3.6 32.6 %copy-start.3 = (bf16[1,1,6,256,256]{4,3,2,1,0:T(8,128)(2,1)S(1)}, bf16[1,1,6,256,256]{4,3,2,1,0:T(8,128)(2,1)}, u32[]{:S(2)}) copy-start(bf16[1,1,6,256,256]{4,3,2,1,0:T(8,128)(2,1)} %param.11) | copy-start | bytes 2359300
  3.6 32.6 %copy-start.5 = (f32[2,136,128]{2,1,0:T(8,128)S(1)}, f32[2,136,128]{2,1,0:T(8,128)}, u32[]{:S(2)}) copy-start(f32[2,136,128]{2,1,0:T(8,128)} %constant.18.clone.twists) | copy-start | bytes 417796
  36.2 1.1 copy-start.4
  37.4 6.3 %copy-start.1 = (f32[2,512,512]{2,1,0:T(8,128)S(1)}, f32[2,512,512]{2,1,0:T(8,128)}, u32[]{:S(2)}) copy-start(f32[2,512,512]{2,1,0:T(8,128)} %field.3) | copy-start | bytes 6291460
